TPU v7x, 256 devices: a whole 4x4x8 slice. The times are simulated.
256 devices in a mesh: frames: 32 (over y, x, core), planes: 8 (over z).
Axes of the slice: x: 4, y: 4, z: 8, core: 2. Of those that a mesh axis runs over, the one named last changes fastest.
Arguments:
- recording: float32 [256, 8, 256, 128], P('frames', 'planes'), may hold values from -30 to 30
- template: float32 [8, 256, 128], P('planes'), may hold values from -4 to 4
- shifts: int32 [256, 8, 2], P('frames', 'planes'), may hold values from -16 to 16
- support: int32 [256, 96], replicated, may hold values from 0 to 255, as said below
- temporal_init: float32 [256, 256], replicated, may hold values from 0 to 0.3
- spatial_init: float32 [256, 8, 32768], P(None, 'planes', 'frames'), may hold values from 0 to 29
Outputs:
- temporal: float32 [256, 256], replicated
- spatial: float32 [256, 8, 32768], P(None, 'planes', 'frames')
Inputs may be any that keep to these rules, and one draw needn't show every extreme that they name: `support`: each component names 96 different tiles.
All inputs are finite; a program needn't handle non-finite values.
Results may differ from a plain program's by a relative error of at most 0.0001.
Values sent between devices are 32-bit elements; how exact they have to be, the bound alone decides.
No kernel may reach another device: no remote copies, remote signals or barrier semaphores. Data moves between devices by JAX's collectives and lax.ppermute only.
A program may use at most 128 MiB of HBM per device.

v0:
```python
import jax
import jax.numpy as jnp
from jax import lax
from jax.sharding import PartitionSpec as P

HEIGHT = 256
WIDTH = 128
TILE = 1024
NTREND = 16


epsilon = 1e-06


def matmul(left_side, right_side):
    return jnp.dot(
        left_side, right_side, precision=lax.Precision.HIGHEST, preferred_element_type=jnp.float32
    )


def cosine_table(frame_count, basis_order):
    times = jnp.arange(frame_count).astype(jnp.float32)
    orders = jnp.arange(basis_order).astype(jnp.float32)
    scales = jnp.where(
        orders == 0, jnp.sqrt(1.0 / frame_count), jnp.sqrt(2.0 / frame_count)
    ).astype(jnp.float32)
    return (
        jnp.cos(jnp.pi * (times[:, None] + 0.5) * orders[None, :] / frame_count) * scales[None, :]
    )


def shift_frame(picture, offsets):
    return jnp.roll(picture, (offsets[0], offsets[1]), axis=(0, 1))


def body(recording, template, shifts, support, temporal_init, spatial_init):
    frame_local = recording.shape[0]
    plane_local = recording.shape[1]
    pixel_count = HEIGHT * WIDTH
    registered = jax.vmap(jax.vmap(shift_frame))(recording, shifts)
    numerator = jnp.sum(registered * template[None], axis=(1, 2, 3))
    energy = jnp.sum(registered * registered, axis=(1, 2, 3))
    template_energy = jnp.sum(template * template)
    flattened = registered.reshape(frame_local, plane_local, pixel_count)
    numerator, energy, template_energy = lax.psum((numerator, energy, template_energy), "planes")
    weight = numerator / jnp.sqrt(energy * template_energy + epsilon)
    payload = flattened * weight[:, None, None]
    series = lax.all_to_all(payload, "frames", split_axis=2, concat_axis=0, tiled=True)
    frames_total = series.shape[0]
    pixels_local = series.shape[2]
    series = series.reshape(frames_total, plane_local * pixels_local)
    cosine_basis = cosine_table(frames_total, NTREND)
    detrended = series - matmul(cosine_basis, matmul(cosine_basis.T, series))
    frame_index = lax.axis_index("frames")
    plane_index = lax.axis_index("planes")
    local_tiles = pixels_local // TILE
    tile_ids = (
        plane_index * (pixel_count // TILE)
        + frame_index * pixels_local // TILE
        + jnp.arange(local_tiles)
    )
    covered = jnp.any(support[:, :, None] == tile_ids[None, None, :], axis=1).astype(jnp.float32)
    components = covered.shape[0]
    support_mask = jnp.broadcast_to(covered[:, :, None], (components, local_tiles, TILE)).reshape(
        components, local_tiles * TILE
    )
    spatial = spatial_init.reshape(components, plane_local * pixels_local) * support_mask
    temporal = temporal_init
    spatial_gram, cross = lax.psum(
        (matmul(spatial, spatial.T), matmul(detrended, spatial.T)), ("frames", "planes")
    )
    temporal_grad = matmul(temporal, spatial_gram) - cross
    grad_square = jnp.sum(temporal_grad * temporal_grad)
    grad_curve = jnp.sum(temporal_grad * matmul(temporal_grad, spatial_gram))
    temporal = jnp.maximum(temporal - grad_square / (grad_curve + epsilon) * temporal_grad, 0.0)
    temporal_gram = matmul(temporal.T, temporal)
    spatial_grad = (matmul(temporal_gram, spatial) - matmul(temporal.T, detrended)) * support_mask
    grad_square, grad_curve = lax.psum(
        (
            jnp.sum(spatial_grad * spatial_grad),
            jnp.sum(spatial_grad * matmul(temporal_gram, spatial_grad)),
        ),
        ("frames", "planes"),
    )
    spatial = jnp.maximum(spatial - grad_square / (grad_curve + epsilon) * spatial_grad, 0.0)
    return (temporal, spatial.reshape(components, plane_local, pixels_local))


def solution(mesh):
    placed = (
        P("frames", "planes", None, None),
        P("planes", None, None),
        P("frames", "planes", None),
        P(),
        P(),
        P(None, "planes", "frames"),
    )
    return jax.shard_map(
        body,
        mesh=mesh,
        in_specs=placed,
        out_specs=(P(), P(None, "planes", "frames")),
        check_vma=False,
    )
```

profile of v0, /device:TPU:1, one launch (start us, length us, event | category | flops | bytes accessed | tf_op | source)
XLA Modules:
  0.0 651.8 jit_solution(1426401225460808278)
XLA Ops:
  7.2 0.8 compare_select_fusion
  7.9 2.3 copy.28
  10.2 1.8 pad_maximum_fusion
  12.1 2.1 gather_fusion
  14.2 1.5 pad_maximum_fusion.1
  15.7 3.8 copy.30
  19.5 0.6 multiply_reduce_fusion.2
  20.2 1.7 gather_fusion.1
  23.0 18.1 %all-reduce.4 = (f32[8]{0:T(128)S(1)}, f32[8]{0:T(128)S(1)}, f32[]{:T(128)}) all-reduce(f32[8]{0:T(128)S(1)} %get-tuple-element.9, f32[8]{0:T(128)S(1)} %get-tuple-element.8, f32[]{:T(128)} %multiply_reduce_fusion.2), channel_id=1, replica_groups=mesh['frames'=32,'planes'=8] {'planes'}, use_global_device_ids=true, to_apply=%region_3.4 | all-reduce | flops 17 | bytes 136 | tf_op jit(solution)/shard_map/psum | solution.py:45
  41.1 0.7 rsqrt_multiply_fusion
  41.9 23.8 %copy.33 = f32[8,1,32768]{0,1,2:T(1,128)} copy(f32[8,1,32768]{2,0,1:T(8,128)S(1)} %broadcast_multiply_fusion.1) | data formatting | bytes 2097152 | tf_op jit(solution)/shard_map/mul | solution.py:47
  66.2 146.5 %reduce.2 = f32[32768,8]{1,0:T(8,128)} reduce(f32[32768,1,8]{2,1,0:T(1,128)} %bitcast.53, f32[]{:T(128)} %broadcast.205), dimensions={1}, to_apply=%bitcast.38.reduce_sub_computation | reduce | bytes 2097156
  212.7 13.0 %reshape.176 = f32[32,1,8192]{2,1,0:T(1,128)} reshape(f32[32768,8]{1,0:T(8,128)} %reduce.2) | data formatting | bytes 2097152
  225.7 11.4 %all-to-all-start = ((f32[32,1,8192]{2,1,0:T(1,128)}), f32[32,1,8192]{2,1,0:T(1,128)S(1)}, u32[]{:S(2)}, u32[]{:S(2)}) async-start(f32[32,1,8192]{2,1,0:T(1,128)} %reshape.176), calls=%async_computation | async-start | bytes 2097152 | tf_op jit(solution)/shard_map/all_to_all | solution.py:48
  237.5 0.8 broadcast_multiply_fusion
  238.3 1.9 fusion.2
  240.2 14.1 %all-to-all-done = f32[32,1,8192]{2,1,0:T(1,128)S(1)} async-done(((f32[32,1,8192]{2,1,0:T(1,128)}), f32[32,1,8192]{2,1,0:T(1,128)S(1)}, u32[]{:S(2)}, u32[]{:S(2)}) %all-to-all-start) | async-done | bytes 1048608 | tf_op jit(solution)/shard_map/all_to_all | solution.py:48
  254.3 3.2 reduce.3
  257.5 32.9 %reshape.177 = f32[32768,1,8]{2,1,0:T(1,128)} reshape(f32[32,8192]{1,0:T(8,128)S(1)} %reduce.3) | data formatting | bytes 2097152
  290.4 10.1 %copy.43 = f32[8,1,32,1024]{3,2,0,1:T(8,128)S(1)} copy(f32[8,1,32,1024]{0,3,2,1:T(8,128)} %bitcast.54) | data formatting | bytes 2097152 | tf_op jit(solution)/shard_map/all_to_all | solution.py:48
  300.6 1.6 fusion.5
  302.2 1.9 convolution_subtract_fusion
  304.1 1.8 fusion.11
  306.1 245.2 %all-reduce.7.cloned.1.call-done = (f32[256,256]{0,1:T(8,128)}, f32[256,256]{1,0:T(8,128)}) async-done(((f32[256,256]{0,1:T(8,128)}, f32[256,256]{1,0:T(8,128)}), (f32[256,256]{0,1:T(8,128)}, f32[256,256]{1,0:T(8,128)})) %all-reduce.7.cloned.1.call-update) | async-done | bytes 524304 | tf_op jit(solution)/shard_map/psum | solution.py:69
  551.3 2.2 multiply_reduce_fusion.1
  553.6 2.2 fusion.13
  557.5 0.8 copy.39
  558.3 1.2 fusion.10
  559.6 1.9 multiply_reduce_fusion
  561.5 1.8 fusion.12
  563.3 77.6 %all-reduce.2 = (f32[]{:T(128)}, f32[]{:T(128)}) all-reduce(f32[]{:T(128)} %get-tuple-element.23, f32[]{:T(128)} %fusion.12), channel_id=1, replica_groups=mesh['frames'=32,'planes'=8] {'frames','planes'}, use_global_device_ids=true, to_apply=%region_12.13 | all-reduce | flops 2 | bytes 16 | tf_op jit(solution)/shard_map/psum | solution.py:78
  642.4 2.0 copy.40
  (33 shorter events, 3.0 us)
Async XLA Ops:
  15.7 3.8 copy-start.4
  225.7 11.7 %copy-start.5 = (s32[256,96]{0,1:T(8,128)S(1)}, s32[256,96]{0,1:T(8,128)}, u32[]{:S(2)}) copy-start(s32[256,96]{0,1:T(8,128)} %param.9) | copy-start | bytes 294916
  225.7 11.8 %copy-start = (f32[256,1,1024]{2,1,0:T(1,128)S(1)}, f32[256,1,1024]{2,1,0:T(1,128)}, u32[]{:S(2)}) copy-start(f32[256,1,1024]{2,1,0:T(1,128)} %param.11) | copy-start | bytes 3145732
  225.7 28.6 %all-to-all-start = ((f32[32,1,8192]{2,1,0:T(1,128)}), f32[32,1,8192]{2,1,0:T(1,128)S(1)}, u32[]{:S(2)}, u32[]{:S(2)}) async-start(f32[32,1,8192]{2,1,0:T(1,128)} %reshape.176), calls=%async_computation | async-start | bytes 2097152 | tf_op jit(solution)/shard_map/all_to_all | solution.py:48
  237.1 314.2 %all-reduce.7.cloned.1.call-start = ((), (), s32[]{:S(2)}) async-start(), calls=%async_computation.1 | async-start | bytes 1048576 | tf_op jit(solution)/shard_map/psum | solution.py:69
  302.2 3.8 copy-start.3
  557.5 0.9 copy-start.1
  559.6 1.9 copy-start.2
Sparse Core Ops, SparseCore 0:
  306.1 245.1 all-reduce.6
where the time goes:
time: 658 us; the launch traced here: 652 us
  waiting for transfers between devices  259 us (39%)
  other arithmetic  157 us (24%)
  blocking collectives  95.8 us (15%)
  local copies, waits for them, and re-layouts  93.9 us (14%)
  between operations  17.3 us (3%)
  matrix products  17 us (3%)
  starting transfers between devices  11.7 us (2%)
    psum x1, waiting for transfers between devices, body(): lax.psum((matmul(spatial, spatial.T), matmul(detrended, spatial.T)), ('fr...  245 us
    unnamed x1, other arithmetic  147 us
    psum x1, blocking collectives, body(): lax.psum((jnp.sum(spatial_grad * spatial_grad), jnp.sum(spatial_grad * ma...  77.6 us
    unnamed x21, local copies, waits for them, and re-layouts  51.8 us
    mul x1, local copies, waits for them, and re-layouts, body(): payload = flattened * weight[:, None, None]  23.8 us
    psum x1, blocking collectives, body(): lax.psum((numerator, energy, template_energy), 'planes')  18.1 us
    dot_general x10, matrix products, matmul(): jnp.dot(left_side, right_side, precision=lax.Precision.HIGHEST, preferred...  17 us
    all_to_all x1, waiting for transfers between devices, body(): lax.all_to_all(payload, 'frames', split_axis=2, concat_axis=0, tiled=True)  14.1 us
  transfers between devices with their start and end apart: 2, of which 2 were waited for; matrix products, arithmetic and copies ran while one was open for 0% of the time, Pallas kernels for 0%

commit v1 on v0

v1 whole, which is shorter than its diff:
```python
import numpy as np
import jax
import jax.numpy as jnp
from jax import lax
from jax.experimental import pallas as pl
from jax.experimental.pallas import tpu as pltpu
from jax.sharding import PartitionSpec as P

HEIGHT = 256
WIDTH = 128
COMP = 256
FRAMES = 256
PLANES = 8
TILE = 1024
NTREND = 16
GROUP = 32
LOCAL = 8
ROWS = TILE // WIDTH
PACK = 640
epsilon = 1e-06

VMEM = pl.BlockSpec(memory_space=pltpu.VMEM)
SMEM = pl.BlockSpec(memory_space=pltpu.SMEM)
PARAMS = pltpu.CompilerParams(vmem_limit_bytes=48 * 1024 * 1024)


def f32(*shape):
    return jax.ShapeDtypeStruct(shape, jnp.float32)


def dot(left, right, dims=((1,), (0,))):
    return lax.dot_general(
        left, right, (dims, ((), ())),
        precision=lax.Precision.HIGHEST, preferred_element_type=jnp.float32,
    )


def cosine_table():
    times = np.arange(FRAMES)[:, None] + 0.5
    orders = np.arange(NTREND)[None, :]
    scales = np.where(orders == 0, np.sqrt(1.0 / FRAMES), np.sqrt(2.0 / FRAMES))
    return (np.cos(np.pi * times * orders / FRAMES) * scales).astype(np.float32)


def register_kernel(shift_ref, movie_ref, out_ref):
    frame = pl.program_id(0)
    down = jnp.mod(shift_ref[0, frame], HEIGHT)
    right = jnp.mod(shift_ref[1, frame], WIDTH)
    picture = pltpu.roll(movie_ref[0], right, 1)
    picture = pltpu.roll(picture, down, 0)
    out_ref[:, 0] = picture.reshape(GROUP, ROWS, WIDTH)


def mask_row(place_ref, support_ref):
    tile = place_ref[1] * GROUP + place_ref[0]
    hits = jnp.where(support_ref[...] == tile, 1.0, 0.0)
    return jnp.max(hits, axis=0, keepdims=True)


def mask_columns(row):
    return jnp.transpose(jnp.broadcast_to(row, (128, COMP)))


def gram_kernel(place_ref, series_ref, spatial_ref, support_ref, template_ref, pack_ref, stack_ref):
    mask = mask_columns(mask_row(place_ref, support_ref))
    start = pl.multiple_of(place_ref[0] * ROWS, ROWS)
    picture = template_ref[pl.ds(start, ROWS), :]
    numerator = jnp.zeros((FRAMES, WIDTH), jnp.float32)
    energy = jnp.zeros((FRAMES, WIDTH), jnp.float32)
    for row in range(ROWS):
        columns = slice(row * WIDTH, (row + 1) * WIDTH)
        series = series_ref[pl.ds(row, FRAMES, stride=ROWS), :]
        spatial = spatial_ref[pl.ds(row, COMP, stride=ROWS), :] * mask
        stack_ref[:COMP, columns] = spatial
        stack_ref[COMP:, columns] = series
        numerator += series * picture[row:row + 1]
        energy += series * series
    products = dot(stack_ref[...], stack_ref[:COMP, :], ((1,), (1,)))
    pack_ref[:, :COMP] = products[:COMP]
    pack_ref[:, COMP:2 * COMP] = products[COMP:]
    lane = lax.broadcasted_iota(jnp.int32, (FRAMES, 128), 1)
    extra = jnp.where(lane == 2, jnp.sum(picture * picture), 0.0)
    extra = jnp.where(lane == 1, jnp.sum(energy, axis=1, keepdims=True), extra)
    extra = jnp.where(lane == 0, jnp.sum(numerator, axis=1, keepdims=True), extra)
    pack_ref[:, 2 * COMP:] = extra


def spread_kernel(in_ref, out_ref):
    total = jnp.sum(in_ref[...], axis=0)
    out_ref[...] = jnp.broadcast_to(total[None], out_ref.shape)


def step_kernel(place_ref, pack_ref, temporal_ref, basis_ref, support_ref, stack_ref,
                out_ref, grad_ref, sums_ref):
    gram = pack_ref[:, :COMP]
    basis = basis_ref[...]

    def detrend(values):
        return values - dot(basis, dot(basis, values, ((0,), (0,))))

    energy = pack_ref[:, 2 * COMP + 1:2 * COMP + 2] * pack_ref[:, 2 * COMP + 2:2 * COMP + 3]
    weight = pack_ref[:, 2 * COMP:2 * COMP + 1] / jnp.sqrt(energy + epsilon)
    cross = detrend(pack_ref[:, COMP:2 * COMP] * weight)
    temporal = temporal_ref[...]
    grad = dot(temporal, gram) - cross
    step = jnp.sum(grad * grad) / (jnp.sum(grad * dot(grad, gram)) + epsilon)
    temporal = jnp.maximum(temporal - step * grad, 0.0)
    out_ref[...] = temporal
    temporal_gram = dot(temporal, temporal, ((0,), (0,)))
    projector = detrend(temporal) * weight
    mask = mask_columns(mask_row(place_ref, support_ref))[:, :1]
    spatial_grad = (
        dot(temporal_gram, stack_ref[:COMP, :]) - dot(projector, stack_ref[COMP:, :], ((0,), (0,)))
    ) * mask
    grad_ref[...] = spatial_grad
    square = jnp.sum(spatial_grad * spatial_grad)
    curve = jnp.sum(spatial_grad * dot(temporal_gram, spatial_grad))
    lane = lax.broadcasted_iota(jnp.int32, sums_ref.shape, 2)
    sums_ref[...] = jnp.where(lane == 0, square, jnp.where(lane == 1, curve, 0.0))


def final_kernel(sums_ref, stack_ref, grad_ref, out_ref):
    totals = jnp.sum(jnp.sum(sums_ref[...], axis=0), axis=0, keepdims=True)
    lane = lax.broadcasted_iota(jnp.int32, totals.shape, 1)
    square = jnp.sum(jnp.where(lane == 0, totals, 0.0))
    curve = jnp.sum(jnp.where(lane == 1, totals, 0.0))
    step = square / (curve + epsilon)
    for row in range(ROWS):
        columns = slice(row * WIDTH, (row + 1) * WIDTH)
        out_ref[pl.ds(row, COMP, stride=ROWS), :] = jnp.maximum(
            stack_ref[:, columns] - step * grad_ref[:, columns], 0.0
        )


def exchange(values, axes):
    return lax.all_to_all(values, axes, split_axis=0, concat_axis=0, tiled=True)


def body(recording, template, shifts, support, temporal_init, spatial_init):
    movie = recording.reshape(LOCAL, HEIGHT, WIDTH)
    shift_table = shifts.transpose(1, 2, 0).reshape(2, LOCAL)
    support_table = support.T
    place = jnp.stack([lax.axis_index("frames"), lax.axis_index("planes")]).astype(jnp.int32)
    payload = pl.pallas_call(
        register_kernel,
        out_shape=f32(GROUP, LOCAL, ROWS, WIDTH),
        grid=(LOCAL,),
        in_specs=[SMEM, pl.BlockSpec((1, HEIGHT, WIDTH), lambda f: (f, 0, 0))],
        out_specs=pl.BlockSpec((GROUP, 1, ROWS, WIDTH), lambda f: (0, f, 0, 0)),
        compiler_params=PARAMS,
        name="register",
    )(shift_table, movie)
    series = exchange(payload, "frames").reshape(FRAMES * ROWS, WIDTH)
    spatial = spatial_init.reshape(COMP * ROWS, WIDTH)
    pack, stack = pl.pallas_call(
        gram_kernel,
        out_shape=(f32(FRAMES, PACK), f32(COMP + FRAMES, TILE)),
        in_specs=[SMEM, VMEM, VMEM, VMEM, VMEM],
        out_specs=(VMEM, VMEM),
        compiler_params=PARAMS,
        name="grams",
    )(place, series, spatial, support_table, template.reshape(HEIGHT, WIDTH))

    def spread(values, copies):
        return pl.pallas_call(
            spread_kernel,
            out_shape=f32(copies, *values.shape[1:]),
            in_specs=[VMEM],
            out_specs=VMEM,
            compiler_params=PARAMS,
            name="spread",
        )(values)

    part = exchange(pack.reshape(GROUP, LOCAL, PACK), "frames")
    part = exchange(spread(part, PLANES), "planes")
    pack = exchange(spread(part, GROUP), "frames").reshape(FRAMES, PACK)
    temporal, grad, sums = pl.pallas_call(
        step_kernel,
        out_shape=(f32(FRAMES, COMP), f32(COMP, TILE), f32(GROUP * PLANES, 1, 128)),
        in_specs=[SMEM] + [VMEM] * 5,
        out_specs=(VMEM, VMEM, VMEM),
        compiler_params=PARAMS,
        name="steps",
    )(place, pack, temporal_init, jnp.asarray(cosine_table()), support_table, stack)
    sums = exchange(sums, ("frames", "planes")).reshape(GROUP, PLANES, 128)
    spatial = pl.pallas_call(
        final_kernel,
        out_shape=f32(COMP * ROWS, WIDTH),
        grid=(1,),
        in_specs=[
            pl.BlockSpec((GROUP, PLANES, 128), lambda i: (0, 0, 0)),
            pl.BlockSpec((COMP, TILE), lambda i: (0, 0)),
            pl.BlockSpec((COMP, TILE), lambda i: (0, 0)),
        ],
        out_specs=pl.BlockSpec((COMP * ROWS, WIDTH), lambda i: (0, 0)),
        compiler_params=PARAMS,
        name="update",
    )(sums, stack, grad)
    return (temporal, spatial.reshape(COMP, 1, TILE))


def solution(mesh):
    placed = (
        P("frames", "planes", None, None),
        P("planes", None, None),
        P("frames", "planes", None),
        P(),
        P(),
        P(None, "planes", "frames"),
    )
    return jax.shard_map(
        body,
        mesh=mesh,
        in_specs=placed,
        out_specs=(P(), P(None, "planes", "frames")),
        check_vma=False,
    )
```

time: 658 us -> 114 us (0.17)
  waiting for transfers between devices: 259 us -> 17.1 us
  other arithmetic: 157 us -> 0.08 us
  local copies, waits for them, and re-layouts: 93.9 us -> 1.92 us
  blocking collectives: 95.8 us -> 70.1 us
  matrix products: 17 us -> 0 us
  between operations: 17.3 us -> 0.7 us
  Pallas kernels: 0 us -> 14.9 us
    psum x1 -> x0, waiting for transfers between devices: 245 us -> none  [body(): lax.psum((matmul(spatial, spatial.T), matmul(detrended, spatial.T)), ('fr...]
    unnamed x1 -> x0, other arithmetic: 147 us -> none
    psum x2 -> x0, blocking collectives: 95.8 us -> none  [the longest x1 77.6 us: body(): lax.psum((jnp.sum(spatial_grad * spatial_grad), jnp.sum(spatial_grad * ma...]
    all_to_all x0 -> x4, blocking collectives: none -> 70.1 us  [exchange(): return lax.all_to_all(values, axes, split_axis=0, concat_axis=0, tiled=True)]
    unnamed x21 -> x14, local copies, waits for them, and re-layouts: 51.8 us -> 1.92 us
    mul x2 -> x0, local copies, waits for them, and re-layouts: 23.9 us -> none  [the longest x1 23.8 us: body(): payload = flattened * weight[:, None, None]]
    dot_general x10 -> x0, matrix products: 17 us -> none  [matmul(): jnp.dot(left_side, right_side, precision=lax.Precision.HIGHEST, preferred...]
    pallas_call x0 -> x6, Pallas kernels: none -> 14.9 us  [the longest x1 6.39 us: body(): pl.pallas_call(step_kernel, out_shape=(f32(FRAMES, COMP), f32(COMP, TILE)...]
  transfers between devices with their start and end apart: 2 -> 1, of which waited for: 2 -> 1; matrix products, arithmetic and copies ran while one was open for 0% -> 0% of each run, Pallas kernels for 0% -> 0%
where the time goes in v1:
time: 114 us; the launch traced here: 113 us
  blocking collectives  70.1 us (61%)
  waiting for transfers between devices  17.1 us (15%)
  Pallas kernels  14.9 us (13%)
  starting transfers between devices  8.59 us (8%)
  local copies, waits for them, and re-layouts  1.92 us (2%)
    all_to_all x4, blocking collectives, exchange(): return lax.all_to_all(values, axes, split_axis=0, concat_axis=0, tiled=True)  70.1 us
    all_to_all x1, waiting for transfers between devices, exchange(): return lax.all_to_all(values, axes, split_axis=0, concat_axis=0, tiled=True)  17.1 us
    all_to_all x1, starting transfers between devices, exchange(): return lax.all_to_all(values, axes, split_axis=0, concat_axis=0, tiled=True)  8.59 us
    pallas_call x1, Pallas kernels, body(): pl.pallas_call(step_kernel, out_shape=(f32(FRAMES, COMP), f32(COMP, TILE)...  6.39 us
    pallas_call x1, Pallas kernels, body(): pl.pallas_call(register_kernel, out_shape=f32(GROUP, LOCAL, ROWS, WIDTH),...  3.85 us
    pallas_call x1, Pallas kernels, body(): pl.pallas_call(gram_kernel, out_shape=(f32(FRAMES, PACK), f32(COMP + FRAM...  2.95 us
  transfers between devices with their start and end apart: 1, of which 1 were waited for; matrix products, arithmetic and copies ran while one was open for 0% of the time, Pallas kernels for 0%

profile of v1, /device:TPU:1, one launch (start us, length us, event | category | flops | bytes accessed | tf_op | source)
XLA Modules:
  0.0 113.4 jit_solution(1556667046813864534)
XLA Ops:
  0.6 0.0 copy-start.1
  0.6 1.2 %copy-done.1 = f32[8,1,256,128]{3,2,1,0:T(8,128)S(1)} copy-done((f32[8,1,256,128]{3,2,1,0:T(8,128)S(1)}, f32[8,1,256,128]{3,2,1,0:T(8,128)}, u32[]{:S(2)}) %copy-start.1) | copy-done | bytes 1048600
  1.9 0.0 copy-start.6
  1.9 0.7 copy-done.6
  2.5 0.0 copy-start
  2.5 0.0 copy-start.2
  2.5 0.0 copy-start.4
  2.5 3.9 %register.1 = f32[32,8,8,128]{3,2,1,0:T(8,128)} custom-call(s32[2,8]{1,0:T(2,128)S(1)} %bitcast.23, f32[8,256,128]{2,1,0:T(8,128)S(1)} %bitcast.17), custom_call_target="tpu_custom_call" | custom-call | tf_op jit(solution)/shard_map/register/pallas_call | solution.py:144
  6.4 8.6 %all-to-all-start = ((f32[32,8,8,128]{3,2,1,0:T(8,128)}), f32[32,8,8,128]{3,2,1,0:T(8,128)S(1)}, u32[]{:S(2)}, u32[]{:S(2)}) async-start(f32[32,8,8,128]{3,2,1,0:T(8,128)} %register.1), calls=%async_computation | async-start | bytes 2097152 | tf_op jit(solution)/shard_map/all_to_all | solution.py:136
  15.0 0.1 pad_add_fusion.place_ref
  15.1 17.1 %all-to-all-done = f32[32,8,8,128]{3,2,1,0:T(8,128)S(1)} async-done(((f32[32,8,8,128]{3,2,1,0:T(8,128)}), f32[32,8,8,128]{3,2,1,0:T(8,128)S(1)}, u32[]{:S(2)}, u32[]{:S(2)}) %all-to-all-start) | async-done | bytes 1048608 | tf_op jit(solution)/shard_map/all_to_all | solution.py:136
  32.2 0.0 copy-done
  32.2 0.0 copy-done.2
  32.2 0.0 copy-done.4
  32.2 2.9 %grams.1 = (f32[256,640]{1,0:T(8,128)S(1)}, f32[512,1024]{1,0:T(8,128)S(1)}) custom-call(s32[2]{0:T(128)S(1)} %pad_add_fusion.place_ref, f32[2048,128]{1,0:T(8,128)S(1)} %bitcast.14, f32[2048,128]{1,0:T(8,128)S(1)} %bitcast.16, s32[96,256]{1,0:T(8,128)S(1)} %bitcast.20, f32[256,128]{1,0:T(8,128)S(1)} %bitcast.22), custom_call_target="tpu_custom_call" | custom-call | tf_op jit(solution)/shard_map/grams/pallas_call | solution.py:155
  35.1 0.0 copy-start.3
  35.1 0.0 copy-start.5
  35.2 16.6 %all_to_all.25.in_ref = f32[32,8,640]{2,1,0:T(8,128)S(1)} all-to-all(f32[32,8,640]{2,1,0:T(8,128)S(1)} %bitcast.18), channel_id=1, replica_groups=mesh['frames'=32,'planes'=8] {'frames'}, dimensions={0} | all-to-all | bytes 1310720 | tf_op jit(solution)/shard_map/all_to_all | solution.py:136
  51.7 0.1 spread.2
  51.8 16.3 %all_to_all.26.in_ref = f32[8,8,640]{2,1,0:T(8,128)S(1)} all-to-all(f32[8,8,640]{2,1,0:T(8,128)S(1)} %spread.2), channel_id=1, replica_groups=mesh['frames'=32,'planes'=8] {'planes'}, dimensions={0} | all-to-all | bytes 327680 | tf_op jit(solution)/shard_map/all_to_all | solution.py:136
  68.1 0.1 spread.3
  68.2 18.7 %all_to_all.27 = f32[32,8,640]{2,1,0:T(8,128)S(1)} all-to-all(f32[32,8,640]{2,1,0:T(8,128)S(1)} %spread.3), channel_id=1, replica_groups=mesh['frames'=32,'planes'=8] {'frames'}, dimensions={0} | all-to-all | bytes 1310720 | tf_op jit(solution)/shard_map/all_to_all | solution.py:136
  86.9 0.0 copy-done.3
  86.9 0.0 copy-done.5
  86.9 6.4 %steps.1 = (f32[256,256]{1,0:T(8,128)}, f32[256,1024]{1,0:T(8,128)S(1)}, f32[256,1,128]{2,1,0:T(1,128)S(1)}) custom-call(s32[2]{0:T(128)S(1)} %pad_add_fusion.place_ref, f32[256,640]{1,0:T(8,128)S(1)} %bitcast.15, f32[256,256]{1,0:T(8,128)S(1)} %copy-done.3, f32[256,16]{1,0:T(8,128)S(1)} %copy-done.5, s32[96,256]{1,0:T(8,128)S(1)} %bitcast.21, ...), custom_call_target="tpu_custom_call" | custom-call | tf_op jit(solution)/shard_map/steps/pallas_call | solution.py:177
  93.3 18.4 %all_to_all.28 = f32[256,1,128]{2,1,0:T(1,128)S(1)} all-to-all(f32[256,1,128]{2,1,0:T(1,128)S(1)} %get-tuple-element.10), channel_id=1, replica_groups=mesh['frames'=32,'planes'=8] {'frames','planes'}, dimensions={0} | all-to-all | bytes 262144 | tf_op jit(solution)/shard_map/all_to_all | solution.py:136
  111.7 1.6 %update.1 = f32[2048,128]{1,0:T(8,128)} custom-call(f32[32,8,128]{2,1,0:T(8,128)S(1)} %bitcast.19, f32[512,1024]{1,0:T(8,128)S(1)} %get-tuple-element.8.stack_ref, f32[256,1024]{1,0:T(8,128)S(1)} %get-tuple-element.11.grad_ref), custom_call_target="tpu_custom_call" | custom-call | tf_op jit(solution)/shard_map/update/pallas_call | solution.py:186
Async XLA Ops:
  0.6 1.2 %copy-start.1 = (f32[8,1,256,128]{3,2,1,0:T(8,128)S(1)}, f32[8,1,256,128]{3,2,1,0:T(8,128)}, u32[]{:S(2)}) copy-start(f32[8,1,256,128]{3,2,1,0:T(8,128)} %param.7) | copy-start | bytes 3145732
  1.9 0.7 copy-start.6
  2.5 29.6 %copy-start = (f32[256,1,1024]{2,1,0:T(1,128)S(1)}, f32[256,1,1024]{2,1,0:T(1,128)}, u32[]{:S(2)}) copy-start(f32[256,1,1024]{2,1,0:T(1,128)} %param.12) | copy-start | bytes 3145732
  2.5 29.6 %copy-start.2 = (s32[256,96]{0,1:T(8,128)S(1)}, s32[256,96]{0,1:T(8,128)}, u32[]{:S(2)}) copy-start(s32[256,96]{0,1:T(8,128)} %param.10) | copy-start | bytes 294916
  2.5 29.6 %copy-start.4 = (f32[1,256,128]{2,1,0:T(8,128)S(1)}, f32[1,256,128]{2,1,0:T(8,128)}, u32[]{:S(2)}) copy-start(f32[1,256,128]{2,1,0:T(8,128)} %param.8) | copy-start | bytes 393220
  6.4 25.8 %all-to-all-start = ((f32[32,8,8,128]{3,2,1,0:T(8,128)}), f32[32,8,8,128]{3,2,1,0:T(8,128)S(1)}, u32[]{:S(2)}, u32[]{:S(2)}) async-start(f32[32,8,8,128]{3,2,1,0:T(8,128)} %register.1), calls=%async_computation | async-start | bytes 2097152 | tf_op jit(solution)/shard_map/all_to_all | solution.py:136
  35.1 51.8 %copy-start.3 = (f32[256,256]{1,0:T(8,128)S(1)}, f32[256,256]{1,0:T(8,128)}, u32[]{:S(2)}) copy-start(f32[256,256]{1,0:T(8,128)} %temporal_ref.1) | copy-start | bytes 786436
  35.1 51.8 %copy-start.5 = (f32[256,16]{1,0:T(8,128)S(1)}, f32[256,16]{1,0:T(8,128)}, u32[]{:S(2)}) copy-start(f32[256,16]{1,0:T(8,128)} %constant.11.clone.basis_ref) | copy-start | bytes 49156

commit v2 on v1

v2 whole, which is shorter than its diff:
```python
import numpy as np
import jax
import jax.numpy as jnp
from jax import lax
from jax.experimental import pallas as pl
from jax.experimental.pallas import tpu as pltpu
from jax.sharding import PartitionSpec as P

HEIGHT = 256
WIDTH = 128
COMP = 256
FRAMES = 256
PLANES = 8
TILE = 1024
NTREND = 16
GROUP = 32
LOCAL = 8
ROWS = TILE // WIDTH
PACK = 512
HALF = 128
MAXS = 16
epsilon = 1e-06

VMEM = pl.BlockSpec(memory_space=pltpu.VMEM)
SMEM = pl.BlockSpec(memory_space=pltpu.SMEM)
HBM = pl.BlockSpec(memory_space=pltpu.HBM)
MIB = 1024 * 1024
NN = ((1,), (0,))
NT = ((1,), (1,))


def f32(*shape):
    return jax.ShapeDtypeStruct(shape, jnp.float32)


def b16(*shape):
    return jax.ShapeDtypeStruct(shape, jnp.bfloat16)


def split(values):
    high = values.astype(jnp.bfloat16)
    return high, (values - high.astype(jnp.float32)).astype(jnp.bfloat16)


def dot(left, right, dims=NN):
    def product(a, b):
        return lax.dot_general(a, b, (dims, ((), ())), preferred_element_type=jnp.float32)

    return product(left[0], right[0]) + (product(left[0], right[1]) + product(left[1], right[0]))


def trend_projector():
    times = np.arange(FRAMES)[:, None] + 0.5
    orders = np.arange(NTREND)[None, :]
    scales = np.where(orders == 0, np.sqrt(1.0 / FRAMES), np.sqrt(2.0 / FRAMES))
    basis = np.cos(np.pi * times * orders / FRAMES) * scales
    return (basis @ basis.T).astype(np.float32)


def register_kernel(shift_hbm, movie_hbm, out_ref, shift_ref, movie_ref, wide_ref, shift_sem, movie_sem):
    table = pltpu.make_async_copy(shift_hbm, shift_ref, shift_sem)
    table.start()
    copies = [
        pltpu.make_async_copy(movie_hbm.at[frame], movie_ref.at[frame], movie_sem.at[frame])
        for frame in range(LOCAL)
    ]
    for copy in copies:
        copy.start()
    table.wait()
    for frame in range(LOCAL):
        copies[frame].wait()
        right = jnp.mod(shift_ref[1, frame], WIDTH)
        picture = pltpu.roll(movie_ref[frame], right, 1)
        wide = wide_ref.at[frame]
        wide[pl.ds(0, MAXS), :] = picture[HEIGHT - MAXS:]
        wide[pl.ds(MAXS, HEIGHT), :] = picture
        wide[pl.ds(MAXS + HEIGHT, MAXS), :] = picture[:MAXS]
        moved = wide[pl.ds(MAXS - shift_ref[0, frame], HEIGHT), :]
        out_ref[:, frame] = moved.reshape(GROUP, ROWS, WIDTH)


def spatial_kernel(place_ref, spatial_ref, support_ref, template_ref,
                   stack_ref, high_ref, low_ref, mask_ref, pack_ref, picture_ref):
    start = pl.multiple_of(place_ref[0] * ROWS, ROWS)
    picture_ref[...] = template_ref[pl.ds(start, ROWS), :]
    tile = place_ref[1] * GROUP + place_ref[0]
    hits = jnp.where(support_ref[...] == tile, 1.0, 0.0)
    covered = jnp.max(hits, axis=0, keepdims=True)
    mask = jnp.transpose(jnp.broadcast_to(covered, (128, COMP)))
    mask_ref[...] = mask
    for row in range(ROWS):
        columns = slice(row * WIDTH, (row + 1) * WIDTH)
        spatial = spatial_ref[pl.ds(row, COMP, stride=ROWS), :] * mask
        stack_ref[:, columns] = spatial
        high_ref[:, columns], low_ref[:, columns] = split(spatial)
    parts = (high_ref[...], low_ref[...])
    gram = dot(parts, parts, NT)
    pack_ref[:HALF, :] = gram[:HALF, :]
    pack_ref[HALF:, :HALF] = gram[HALF:, HALF:]
    pack_ref[HALF:, HALF:] = pltpu.roll(gram[:HALF, HALF:], HALF // 2, 1)


def cross_kernel(series_ref, picture_ref, spatial_high_ref, spatial_low_ref, gram_ref,
                 pack_ref, high_ref, low_ref):
    picture = picture_ref[...]
    numerator = jnp.zeros((FRAMES, WIDTH), jnp.float32)
    energy = jnp.zeros((FRAMES, WIDTH), jnp.float32)
    for row in range(ROWS):
        columns = slice(row * WIDTH, (row + 1) * WIDTH)
        series = series_ref[pl.ds(row, FRAMES, stride=ROWS), :]
        high_ref[:, columns], low_ref[:, columns] = split(series)
        numerator += series * picture[row:row + 1]
        energy += series * series
    lane = lax.broadcasted_iota(jnp.int32, (FRAMES, 128), 1)
    extra = jnp.where(lane == HALF // 2, jnp.sum(numerator, axis=1, keepdims=True), jnp.sum(picture * picture))
    extra = jnp.where(lane == HALF // 2 + 1, jnp.sum(energy, axis=1, keepdims=True), extra)
    pack_ref[:, :HALF] = gram_ref[:, :HALF]
    pack_ref[:, HALF:2 * HALF] = jnp.where(lane < HALF // 2, gram_ref[:, HALF:], extra)
    pack_ref[:, COMP:] = dot(
        (high_ref[...], low_ref[...]), (spatial_high_ref[...], spatial_low_ref[...]), NT
    )


def spread_kernel(in_ref, out_ref):
    total = jnp.sum(in_ref[...], axis=0)
    out_ref[...] = jnp.broadcast_to(total[None], out_ref.shape)


def step_kernel(pack_ref, temporal_ref, trend_ref, mask_ref, spatial_high_ref, spatial_low_ref,
                high_ref, low_ref, out_ref, grad_ref, sums_ref):
    lane = lax.broadcasted_iota(jnp.int32, (HALF, HALF), 1)
    corner = jnp.where(
        lane < HALF // 2,
        pack_ref[:HALF, HALF:2 * HALF],
        pltpu.roll(pack_ref[HALF:, HALF:2 * HALF], HALF // 2, 1),
    )
    gram = split(jnp.concatenate([
        jnp.concatenate([pack_ref[:HALF, :HALF], corner], axis=1),
        jnp.concatenate([jnp.transpose(corner), pack_ref[HALF:, :HALF]], axis=1),
    ], axis=0))
    extra = pack_ref[:, HALF:2 * HALF]
    first = HALF // 2
    energy = extra[:, first + 1:first + 2] * extra[:, first + 2:first + 3]
    weight = extra[:, first:first + 1] / jnp.sqrt(energy + epsilon)
    trend = split(trend_ref[...])
    cross = pack_ref[:, COMP:] * weight
    cross = cross - dot(trend, split(cross))
    temporal = temporal_ref[...]
    grad = dot(split(temporal), gram) - cross
    step = jnp.sum(grad * grad) / (jnp.sum(grad * dot(split(grad), gram)) + epsilon)
    temporal = jnp.maximum(temporal - step * grad, 0.0)
    out_ref[...] = temporal
    flipped = jnp.transpose(temporal)
    parts = split(flipped)
    temporal_gram = split(dot(parts, parts, NT))
    weight_row = jnp.transpose(jnp.broadcast_to(weight, (FRAMES, 128)))[:1]
    projector = split((flipped - dot(parts, trend)) * weight_row)
    spatial_grad = (
        dot(temporal_gram, (spatial_high_ref[...], spatial_low_ref[...]))
        - dot(projector, (high_ref[...], low_ref[...]))
    ) * mask_ref[:, :1]
    grad_ref[...] = spatial_grad
    square = jnp.sum(spatial_grad * spatial_grad)
    curve = jnp.sum(spatial_grad * dot(temporal_gram, split(spatial_grad)))
    lane = lax.broadcasted_iota(jnp.int32, sums_ref.shape, 2)
    sums_ref[...] = jnp.where(lane == 0, square, jnp.where(lane == 1, curve, 0.0))


BLOCKS = 4


def final_kernel(sums_ref, stack_ref, grad_ref, out_ref):
    totals = jnp.sum(jnp.sum(sums_ref[...], axis=0), axis=0, keepdims=True)
    lane = lax.broadcasted_iota(jnp.int32, totals.shape, 1)
    square = jnp.sum(jnp.where(lane == 0, totals, 0.0))
    curve = jnp.sum(jnp.where(lane == 1, totals, 0.0))
    step = square / (curve + epsilon)
    size = COMP // BLOCKS
    rows = pl.ds(pl.multiple_of(pl.program_id(0) * size, size), size)
    for row in range(ROWS):
        columns = pl.ds(row * WIDTH, WIDTH)
        out_ref[pl.ds(row, size, stride=ROWS), :] = jnp.maximum(
            stack_ref[rows, columns] - step * grad_ref[rows, columns], 0.0
        )


def exchange(values, axes):
    return lax.all_to_all(values, axes, split_axis=0, concat_axis=0, tiled=True)


def call(kernel, name, out_shape, in_specs, cost=None, vmem=24, **options):
    single = not isinstance(out_shape, tuple)
    options.setdefault("out_specs", VMEM if single else (VMEM,) * len(out_shape))
    return pl.pallas_call(
        kernel, out_shape=out_shape, in_specs=in_specs, name=name, cost_estimate=cost,
        compiler_params=pltpu.CompilerParams(vmem_limit_bytes=vmem * MIB), **options,
    )


def body(recording, template, shifts, support, temporal_init, spatial_init):
    movie = recording.reshape(LOCAL, HEIGHT, WIDTH)
    shift_table = shifts.transpose(1, 2, 0).reshape(2, LOCAL)
    place = jnp.stack([lax.axis_index("frames"), lax.axis_index("planes")]).astype(jnp.int32)
    payload = call(
        register_kernel, "register", f32(GROUP, LOCAL, ROWS, WIDTH), [HBM, HBM], vmem=60,
        scratch_shapes=[
            pltpu.SMEM((2, LOCAL), jnp.int32),
            pltpu.VMEM((LOCAL, HEIGHT, WIDTH), jnp.float32),
            pltpu.VMEM((LOCAL, HEIGHT + 2 * MAXS, WIDTH), jnp.float32),
            pltpu.SemaphoreType.DMA,
            pltpu.SemaphoreType.DMA((LOCAL,)),
        ],
    )(shift_table, movie)
    series = exchange(payload, "frames").reshape(FRAMES * ROWS, WIDTH)
    spatial = spatial_init.reshape(COMP * ROWS, WIDTH)
    stack, spatial_high, spatial_low, mask, gram, picture = call(
        spatial_kernel, "spatial",
        (f32(COMP, TILE), b16(COMP, TILE), b16(COMP, TILE), f32(COMP, 128), f32(COMP, COMP),
         f32(ROWS, WIDTH)),
        [SMEM] + [VMEM] * 3,
        cost=pl.CostEstimate(flops=6 * COMP * COMP * TILE, bytes_accessed=4 << 20, transcendentals=0),
    )(place, spatial, support.T, template.reshape(HEIGHT, WIDTH))
    pack, high, low = call(
        cross_kernel, "cross", (f32(FRAMES, PACK), b16(FRAMES, TILE), b16(FRAMES, TILE)),
        [VMEM] * 5,
    )(series, picture, spatial_high, spatial_low, gram)

    def spread(values, copies):
        return call(spread_kernel, "spread", f32(copies, *values.shape[1:]), [VMEM])(values)

    part = exchange(pack.reshape(GROUP, LOCAL, PACK), "frames")
    part = exchange(spread(part, PLANES), "planes")
    pack = exchange(spread(part, GROUP), "frames").reshape(FRAMES, PACK)
    temporal, grad, sums = call(
        step_kernel, "steps",
        (f32(FRAMES, COMP), f32(COMP, TILE), f32(GROUP * PLANES, 1, 128)),
        [VMEM] * 8,
    )(pack, temporal_init, jnp.asarray(trend_projector()), mask, spatial_high, spatial_low, high, low)
    sums = exchange(sums, ("frames", "planes")).reshape(GROUP, PLANES, 128)
    spatial = call(
        final_kernel, "update", f32(COMP * ROWS, WIDTH), [VMEM] * 3,
        grid=(BLOCKS,),
        out_specs=pl.BlockSpec((COMP * ROWS // BLOCKS, WIDTH), lambda i: (i, 0)),
    )(sums, stack, grad)
    return (temporal, spatial.reshape(COMP, 1, TILE))


def solution(mesh):
    placed = (
        P("frames", "planes", None, None),
        P("planes", None, None),
        P("frames", "planes", None),
        P(),
        P(),
        P(None, "planes", "frames"),
    )
    return jax.shard_map(
        body,
        mesh=mesh,
        in_specs=placed,
        out_specs=(P(), P(None, "planes", "frames")),
        check_vma=False,
    )
```

time: 114 us -> 103 us (0.904)
  waiting for transfers between devices: 17.1 us -> 12.6 us
  Pallas kernels: 14.9 us -> 11.3 us
  blocking collectives: 70.1 us -> 66.5 us
    all_to_all x1, waiting for transfers between devices: 17.1 us -> 12.6 us  [exchange(): return lax.all_to_all(values, axes, split_axis=0, concat_axis=0, tiled=True)]
    all_to_all x4, blocking collectives: 70.1 us -> 66.5 us  [exchange(): return lax.all_to_all(values, axes, split_axis=0, concat_axis=0, tiled=True)]
    pallas_call x6 -> x7, Pallas kernels: 14.9 us -> 11.3 us  [the longest x1 3.83 us: body(): call(step_kernel, 'steps', (f32(FRAMES, COMP), f32(COMP, TILE), f32(GROUP...]
    unnamed x14 -> x10, local copies, waits for them, and re-layouts: 1.92 us -> 3.03 us
  transfers between devices with their start and end apart: 1 -> 1, of which waited for: 1 -> 1; matrix products, arithmetic and copies ran while one was open for 0% -> 0% of each run, Pallas kernels for 0% -> 1%
where the time goes in v2:
time: 103 us
  blocking collectives  66.5 us (65%)
  waiting for transfers between devices  12.6 us (12%)
  Pallas kernels  11.3 us (11%)
  starting transfers between devices  8.6 us (8%)
  local copies, waits for them, and re-layouts  3.03 us (3%)
    all_to_all x4, blocking collectives, exchange(): return lax.all_to_all(values, axes, split_axis=0, concat_axis=0, tiled=True)  66.5 us
    all_to_all x1, waiting for transfers between devices, exchange(): return lax.all_to_all(values, axes, split_axis=0, concat_axis=0, tiled=True)  12.6 us
    all_to_all x1, starting transfers between devices, exchange(): return lax.all_to_all(values, axes, split_axis=0, concat_axis=0, tiled=True)  8.6 us
    pallas_call x1, Pallas kernels, body(): call(step_kernel, 'steps', (f32(FRAMES, COMP), f32(COMP, TILE), f32(GROUP...  3.83 us
    unnamed x10, local copies, waits for them, and re-layouts  3.03 us
    pallas_call x1, Pallas kernels, body(): call(register_kernel, 'register', f32(GROUP, LOCAL, ROWS, WIDTH), [HBM, H...  2.96 us
    pallas_call x1, Pallas kernels, body(): call(final_kernel, 'update', f32(COMP * ROWS, WIDTH), [VMEM] * 3, grid=(B...  2.21 us
  transfers between devices with their start and end apart: 1, of which 1 were waited for; matrix products, arithmetic and copies ran while one was open for 0% of the time, Pallas kernels for 1%

profile of v2, /device:TPU:1, one launch (start us, length us, event | category | flops | bytes accessed | tf_op | source)
XLA Modules:
  0.0 102.8 jit_solution(11538763882340949221)
XLA Ops:
  0.6 3.0 %register.1 = f32[32,8,8,128]{3,2,1,0:T(8,128)} custom-call(s32[2,8]{1,0:T(2,128)} %bitcast.23, f32[8,256,128]{2,1,0:T(8,128)} %bitcast.22), custom_call_target="tpu_custom_call" | custom-call | tf_op jit(solution)/shard_map/register/pallas_call | solution.py:204
  3.6 8.6 %all-to-all-start = ((f32[32,8,8,128]{3,2,1,0:T(8,128)}), f32[32,8,8,128]{3,2,1,0:T(8,128)S(1)}, u32[]{:S(2)}, u32[]{:S(2)}) async-start(f32[32,8,8,128]{3,2,1,0:T(8,128)} %register.1), calls=%async_computation | async-start | bytes 2097152 | tf_op jit(solution)/shard_map/all_to_all | solution.py:188
  12.2 0.1 pad_add_fusion.place_ref
  12.3 0.0 copy-start.2
  12.3 1.2 %copy-done.2 = f32[256,1,1024]{2,1,0:T(1,128)S(1)} copy-done((f32[256,1,1024]{2,1,0:T(1,128)S(1)}, f32[256,1,1024]{2,1,0:T(1,128)}, u32[]{:S(2)}) %copy-start.2) | copy-done | bytes 1048600
  13.5 0.0 copy-start.3
  13.5 0.9 copy-done.3
  14.4 0.0 copy-start.4
  14.4 0.9 copy-done.4
  15.3 1.5 %spatial.1 = (f32[256,1024]{1,0:T(8,128)S(1)}, bf16[256,1024]{1,0:T(8,128)(2,1)S(1)}, bf16[256,1024]{1,0:T(8,128)(2,1)S(1)}, f32[256,128]{1,0:T(8,128)S(1)}, f32...) custom-call(s32[2]{0:T(128)S(1)} %pad_add_fusion.place_ref, f32[2048,128]{1,0:T(8,128)S(1)} %bitcast.18, ...), custom_call_target="tpu_custom_call" | custom-call | flops 402653184 | bytes 4194304 | tf_op jit(solution)/shard_map/spatial/pallas_call | solution.py:216
  16.8 12.6 %all-to-all-done = f32[32,8,8,128]{3,2,1,0:T(8,128)S(1)} async-done(((f32[32,8,8,128]{3,2,1,0:T(8,128)}), f32[32,8,8,128]{3,2,1,0:T(8,128)S(1)}, u32[]{:S(2)}, u32[]{:S(2)}) %all-to-all-start) | async-done | bytes 1048608 | tf_op jit(solution)/shard_map/all_to_all | solution.py:188
  29.4 0.7 cross.1
  30.1 15.1 %all_to_all.25.in_ref = f32[32,8,512]{2,1,0:T(8,128)S(1)} all-to-all(f32[32,8,512]{2,1,0:T(8,128)S(1)} %bitcast.17), channel_id=1, replica_groups=mesh['frames'=32,'planes'=8] {'frames'}, dimensions={0} | all-to-all | bytes 1048576 | tf_op jit(solution)/shard_map/all_to_all | solution.py:188
  45.2 15.8 %all_to_all.26.in_ref = f32[8,8,512]{2,1,0:T(8,128)S(1)} all-to-all(f32[8,8,512]{2,1,0:T(8,128)S(1)} %spread.2), channel_id=1, replica_groups=mesh['frames'=32,'planes'=8] {'planes'}, dimensions={0} | all-to-all | bytes 262144 | tf_op jit(solution)/shard_map/all_to_all | solution.py:188
  61.0 0.1 spread.3
  61.0 0.0 copy-start
  61.1 0.0 copy-start.1
  61.1 17.3 %all_to_all.27 = f32[32,8,512]{2,1,0:T(8,128)S(1)} all-to-all(f32[32,8,512]{2,1,0:T(8,128)S(1)} %spread.3), channel_id=1, replica_groups=mesh['frames'=32,'planes'=8] {'frames'}, dimensions={0} | all-to-all | bytes 1048576 | tf_op jit(solution)/shard_map/all_to_all | solution.py:188
  78.4 0.0 copy-done
  78.4 0.0 copy-done.1
  78.4 3.8 %steps.1 = (f32[256,256]{1,0:T(8,128)}, f32[256,1024]{1,0:T(8,128)S(1)}, f32[256,1,128]{2,1,0:T(1,128)S(1)}) custom-call(f32[256,512]{1,0:T(8,128)S(1)} %bitcast.15, f32[256,256]{1,0:T(8,128)S(1)} %copy-done, f32[256,256]{1,0:T(8,128)S(1)} %copy-done.1, f32[256,128]{1,0:T(8,128)S(1)} %get-tuple-element.19.mask_ref, ...), custom_call_target="tpu_custom_call" | custom-call | tf_op jit(solution)/shard_map/steps/pallas_call | solution.py:234
  82.2 18.3 %all_to_all.28 = f32[256,1,128]{2,1,0:T(1,128)S(1)} all-to-all(f32[256,1,128]{2,1,0:T(1,128)S(1)} %get-tuple-element.23), channel_id=1, replica_groups=mesh['frames'=32,'planes'=8] {'frames','planes'}, dimensions={0} | all-to-all | bytes 262144 | tf_op jit(solution)/shard_map/all_to_all | solution.py:188
  100.6 2.2 %update.1 = f32[2048,128]{1,0:T(8,128)} custom-call(f32[32,8,128]{2,1,0:T(8,128)S(1)} %bitcast.16, f32[256,1024]{1,0:T(8,128)S(1)} %get-tuple-element.24.stack_ref, f32[256,1024]{1,0:T(8,128)S(1)} %get-tuple-element.25.grad_ref), custom_call_target="tpu_custom_call" | custom-call | tf_op jit(solution)/shard_map/update/pallas_call | solution.py:240
  (1 shorter events, 0.0 us)
Async XLA Ops:
  3.6 25.8 %all-to-all-start = ((f32[32,8,8,128]{3,2,1,0:T(8,128)}), f32[32,8,8,128]{3,2,1,0:T(8,128)S(1)}, u32[]{:S(2)}, u32[]{:S(2)}) async-start(f32[32,8,8,128]{3,2,1,0:T(8,128)} %register.1), calls=%async_computation | async-start | bytes 2097152 | tf_op jit(solution)/shard_map/all_to_all | solution.py:188
  12.3 1.2 %copy-start.2 = (f32[256,1,1024]{2,1,0:T(1,128)S(1)}, f32[256,1,1024]{2,1,0:T(1,128)}, u32[]{:S(2)}) copy-start(f32[256,1,1024]{2,1,0:T(1,128)} %param.12) | copy-start | bytes 3145732
  13.5 0.9 copy-start.3
  14.4 0.9 copy-start.4
  61.0 17.4 %copy-start = (f32[256,256]{1,0:T(8,128)S(1)}, f32[256,256]{1,0:T(8,128)}, u32[]{:S(2)}) copy-start(f32[256,256]{1,0:T(8,128)} %temporal_ref.1) | copy-start | bytes 786436
  61.1 17.3 %copy-start.1 = (f32[256,256]{1,0:T(8,128)S(1)}, f32[256,256]{1,0:T(8,128)}, u32[]{:S(2)}) copy-start(f32[256,256]{1,0:T(8,128)} %constant.11.clone.trend_ref) | copy-start | bytes 786436

commit v3 on v2

--- a/solution.py
+++ b/solution.py
@@ -57,7 +57,8 @@
     return (basis @ basis.T).astype(np.float32)
 
 
-def register_kernel(shift_hbm, movie_hbm, out_ref, shift_ref, movie_ref, wide_ref, shift_sem, movie_sem):
+def register_kernel(shift_hbm, movie_hbm, out_hbm, shift_ref, movie_ref, wide_ref, moved_ref,
+                    shift_sem, movie_sem, moved_sem):
     table = pltpu.make_async_copy(shift_hbm, shift_ref, shift_sem)
     table.start()
     copies = [
@@ -67,6 +68,7 @@
     for copy in copies:
         copy.start()
     table.wait()
+    stores = []
     for frame in range(LOCAL):
         copies[frame].wait()
         right = jnp.mod(shift_ref[1, frame], WIDTH)
@@ -76,7 +78,13 @@
         wide[pl.ds(MAXS, HEIGHT), :] = picture
         wide[pl.ds(MAXS + HEIGHT, MAXS), :] = picture[:MAXS]
         moved = wide[pl.ds(MAXS - shift_ref[0, frame], HEIGHT), :]
-        out_ref[:, frame] = moved.reshape(GROUP, ROWS, WIDTH)
+        moved_ref[frame] = moved.reshape(GROUP, ROWS, WIDTH)
+        stores.append(
+            pltpu.make_async_copy(moved_ref.at[frame], out_hbm.at[:, frame], moved_sem.at[frame])
+        )
+        stores[frame].start()
+    for store in stores:
+        store.wait()
 
 
 def spatial_kernel(place_ref, spatial_ref, support_ref, template_ref,
@@ -91,7 +99,7 @@
     for row in range(ROWS):
         columns = slice(row * WIDTH, (row + 1) * WIDTH)
         spatial = spatial_ref[pl.ds(row, COMP, stride=ROWS), :] * mask
-        stack_ref[:, columns] = spatial
+        stack_ref[pl.ds(row, COMP, stride=ROWS), :] = spatial
         high_ref[:, columns], low_ref[:, columns] = split(spatial)
     parts = (high_ref[...], low_ref[...])
     gram = dot(parts, parts, NT)
@@ -100,8 +108,8 @@
     pack_ref[HALF:, HALF:] = pltpu.roll(gram[:HALF, HALF:], HALF // 2, 1)
 
 
-def cross_kernel(series_ref, picture_ref, spatial_high_ref, spatial_low_ref, gram_ref,
-                 pack_ref, high_ref, low_ref):
+def cross_kernel(core_ref, series_ref, picture_ref, spatial_high_ref, spatial_low_ref, gram_ref,
+                 keep_ref, give_ref, high_ref, low_ref, pack_ref):
     picture = picture_ref[...]
     numerator = jnp.zeros((FRAMES, WIDTH), jnp.float32)
     energy = jnp.zeros((FRAMES, WIDTH), jnp.float32)
@@ -119,6 +127,14 @@
     pack_ref[:, COMP:] = dot(
         (high_ref[...], low_ref[...]), (spatial_high_ref[...], spatial_low_ref[...]), NT
     )
+    mine = pl.multiple_of(core_ref[2] * HALF, HALF)
+    other = pl.multiple_of(HALF - core_ref[2] * HALF, HALF)
+    keep_ref[...] = pack_ref[pl.ds(mine, HALF), :]
+    give_ref[...] = pack_ref[pl.ds(other, HALF), :]
+
+
+def add_kernel(left_ref, right_ref, out_ref):
+    out_ref[...] = left_ref[...] + right_ref[...]
 
 
 def spread_kernel(in_ref, out_ref):
@@ -126,8 +142,13 @@
     out_ref[...] = jnp.broadcast_to(total[None], out_ref.shape)
 
 
-def step_kernel(pack_ref, temporal_ref, trend_ref, mask_ref, spatial_high_ref, spatial_low_ref,
-                high_ref, low_ref, out_ref, grad_ref, sums_ref):
+def step_kernel(core_ref, mine_ref, other_ref, temporal_ref, trend_ref, mask_ref,
+                spatial_high_ref, spatial_low_ref, high_ref, low_ref,
+                out_ref, grad_ref, sums_ref, pack_ref):
+    mine = pl.multiple_of(core_ref[2] * HALF, HALF)
+    other = pl.multiple_of(HALF - core_ref[2] * HALF, HALF)
+    pack_ref[pl.ds(mine, HALF), :] = mine_ref[...]
+    pack_ref[pl.ds(other, HALF), :] = other_ref[...]
     lane = lax.broadcasted_iota(jnp.int32, (HALF, HALF), 1)
     corner = jnp.where(
         lane < HALF // 2,
@@ -159,7 +180,8 @@
         dot(temporal_gram, (spatial_high_ref[...], spatial_low_ref[...]))
         - dot(projector, (high_ref[...], low_ref[...]))
     ) * mask_ref[:, :1]
-    grad_ref[...] = spatial_grad
+    for row in range(ROWS):
+        grad_ref[pl.ds(row, COMP, stride=ROWS), :] = spatial_grad[:, row * WIDTH:(row + 1) * WIDTH]
     square = jnp.sum(spatial_grad * spatial_grad)
     curve = jnp.sum(spatial_grad * dot(temporal_gram, split(spatial_grad)))
     lane = lax.broadcasted_iota(jnp.int32, sums_ref.shape, 2)
@@ -169,23 +191,31 @@
 BLOCKS = 4
 
 
-def final_kernel(sums_ref, stack_ref, grad_ref, out_ref):
+def final_kernel(sums_ref, stack_ref, grad_ref, out_hbm, out_ref, sems):
     totals = jnp.sum(jnp.sum(sums_ref[...], axis=0), axis=0, keepdims=True)
     lane = lax.broadcasted_iota(jnp.int32, totals.shape, 1)
     square = jnp.sum(jnp.where(lane == 0, totals, 0.0))
     curve = jnp.sum(jnp.where(lane == 1, totals, 0.0))
     step = square / (curve + epsilon)
-    size = COMP // BLOCKS
-    rows = pl.ds(pl.multiple_of(pl.program_id(0) * size, size), size)
-    for row in range(ROWS):
-        columns = pl.ds(row * WIDTH, WIDTH)
-        out_ref[pl.ds(row, size, stride=ROWS), :] = jnp.maximum(
-            stack_ref[rows, columns] - step * grad_ref[rows, columns], 0.0
-        )
-
-
-def exchange(values, axes):
-    return lax.all_to_all(values, axes, split_axis=0, concat_axis=0, tiled=True)
+    size = COMP * ROWS // BLOCKS
+    stores = []
+    for block in range(BLOCKS):
+        rows = pl.ds(block * size, size)
+        out_ref[rows, :] = jnp.maximum(stack_ref[rows, :] - step * grad_ref[rows, :], 0.0)
+        stores.append(pltpu.make_async_copy(out_ref.at[rows], out_hbm.at[rows], sems.at[block]))
+        stores[block].start()
+    for store in stores:
+        store.wait()
+
+
+def exchange(values, axes, groups=None):
+    return lax.all_to_all(
+        values, axes, split_axis=0, concat_axis=0, axis_index_groups=groups, tiled=True
+    )
+
+
+def swap(values):
+    return lax.ppermute(values, "frames", [(index, index ^ 1) for index in range(GROUP)])
 
 
 def call(kernel, name, out_shape, in_specs, cost=None, vmem=24, **options):
@@ -200,14 +230,17 @@
 def body(recording, template, shifts, support, temporal_init, spatial_init):
     movie = recording.reshape(LOCAL, HEIGHT, WIDTH)
     shift_table = shifts.transpose(1, 2, 0).reshape(2, LOCAL)
-    place = jnp.stack([lax.axis_index("frames"), lax.axis_index("planes")]).astype(jnp.int32)
+    index = lax.axis_index("frames")
+    place = jnp.stack([index, lax.axis_index("planes"), index & 1]).astype(jnp.int32)
     payload = call(
-        register_kernel, "register", f32(GROUP, LOCAL, ROWS, WIDTH), [HBM, HBM], vmem=60,
+        register_kernel, "register", f32(GROUP, LOCAL, ROWS, WIDTH), [HBM, HBM], vmem=60, out_specs=HBM,
         scratch_shapes=[
             pltpu.SMEM((2, LOCAL), jnp.int32),
             pltpu.VMEM((LOCAL, HEIGHT, WIDTH), jnp.float32),
             pltpu.VMEM((LOCAL, HEIGHT + 2 * MAXS, WIDTH), jnp.float32),
+            pltpu.VMEM((LOCAL, GROUP, ROWS, WIDTH), jnp.float32),
             pltpu.SemaphoreType.DMA,
+            pltpu.SemaphoreType.DMA((LOCAL,)),
             pltpu.SemaphoreType.DMA((LOCAL,)),
         ],
     )(shift_table, movie)
@@ -215,32 +248,39 @@
     spatial = spatial_init.reshape(COMP * ROWS, WIDTH)
     stack, spatial_high, spatial_low, mask, gram, picture = call(
         spatial_kernel, "spatial",
-        (f32(COMP, TILE), b16(COMP, TILE), b16(COMP, TILE), f32(COMP, 128), f32(COMP, COMP),
+        (f32(COMP * ROWS, WIDTH), b16(COMP, TILE), b16(COMP, TILE), f32(COMP, 128), f32(COMP, COMP),
          f32(ROWS, WIDTH)),
         [SMEM] + [VMEM] * 3,
         cost=pl.CostEstimate(flops=6 * COMP * COMP * TILE, bytes_accessed=4 << 20, transcendentals=0),
     )(place, spatial, support.T, template.reshape(HEIGHT, WIDTH))
-    pack, high, low = call(
-        cross_kernel, "cross", (f32(FRAMES, PACK), b16(FRAMES, TILE), b16(FRAMES, TILE)),
-        [VMEM] * 5,
-    )(series, picture, spatial_high, spatial_low, gram)
+    keep, give, high, low = call(
+        cross_kernel, "cross",
+        (f32(HALF, PACK), f32(HALF, PACK), b16(FRAMES, TILE), b16(FRAMES, TILE)),
+        [SMEM] + [VMEM] * 5,
+        scratch_shapes=[pltpu.VMEM((FRAMES, PACK), jnp.float32)],
+    )(place, series, picture, spatial_high, spatial_low, gram)
 
     def spread(values, copies):
         return call(spread_kernel, "spread", f32(copies, *values.shape[1:]), [VMEM])(values)
 
-    part = exchange(pack.reshape(GROUP, LOCAL, PACK), "frames")
+    chips = [list(range(core, GROUP, 2)) for core in range(2)]
+    part = call(add_kernel, "pair", f32(HALF, PACK), [VMEM] * 2)(keep, swap(give))
+    part = exchange(part.reshape(GROUP // 2, LOCAL, PACK), "frames", chips)
     part = exchange(spread(part, PLANES), "planes")
-    pack = exchange(spread(part, GROUP), "frames").reshape(FRAMES, PACK)
+    mine = exchange(spread(part, GROUP // 2), "frames", chips).reshape(HALF, PACK)
     temporal, grad, sums = call(
         step_kernel, "steps",
-        (f32(FRAMES, COMP), f32(COMP, TILE), f32(GROUP * PLANES, 1, 128)),
-        [VMEM] * 8,
-    )(pack, temporal_init, jnp.asarray(trend_projector()), mask, spatial_high, spatial_low, high, low)
+        (f32(FRAMES, COMP), f32(COMP * ROWS, WIDTH), f32(GROUP * PLANES, 1, 128)),
+        [SMEM] + [VMEM] * 9,
+        scratch_shapes=[pltpu.VMEM((FRAMES, PACK), jnp.float32)],
+    )(place, mine, swap(mine), temporal_init, jnp.asarray(trend_projector()), mask,
+      spatial_high, spatial_low, high, low)
     sums = exchange(sums, ("frames", "planes")).reshape(GROUP, PLANES, 128)
     spatial = call(
-        final_kernel, "update", f32(COMP * ROWS, WIDTH), [VMEM] * 3,
-        grid=(BLOCKS,),
-        out_specs=pl.BlockSpec((COMP * ROWS // BLOCKS, WIDTH), lambda i: (i, 0)),
+        final_kernel, "update", f32(COMP * ROWS, WIDTH), [VMEM] * 3, out_specs=HBM,
+        scratch_shapes=[
+            pltpu.VMEM((COMP * ROWS, WIDTH), jnp.float32), pltpu.SemaphoreType.DMA((BLOCKS,)),
+        ],
     )(sums, stack, grad)
     return (temporal, spatial.reshape(COMP, 1, TILE))
 

time: 103 us -> 99.5 us (0.966)
  blocking collectives: 66.5 us -> 56.2 us
  starting transfers between devices: 8.6 us -> 12.9 us
  waiting for transfers between devices: 12.6 us -> 14.7 us
    all_to_all x4, blocking collectives: 66.5 us -> 56.2 us  [exchange(): lax.all_to_all(values, axes, split_axis=0, concat_axis=0, axis_index_grou...]
    ppermute x0 -> x2, starting transfers between devices: none -> 4.33 us  [swap(): lax.ppermute(values, 'frames', [(index, index ^ 1) for index in range(GRO...]
    ppermute x0 -> x2, waiting for transfers between devices: none -> 2.32 us  [swap(): lax.ppermute(values, 'frames', [(index, index ^ 1) for index in range(GRO...]
    pallas_call x4 -> x5, Pallas kernels: 8.29 us -> 8.73 us  [the longest x1 4.44 us: body(): call(step_kernel, 'steps', (f32(FRAMES, COMP), f32(COMP * ROWS, WIDTH), f...]
  transfers between devices with their start and end apart: 1 -> 3, of which waited for: 1 -> 3; matrix products, arithmetic and copies ran while one was open for 0% -> 0% of each run, Pallas kernels for 1% -> 2%
where the time goes in v3:
time: 99.5 us; the launch traced here: 99.1 us
  blocking collectives  56.2 us (56%)
  waiting for transfers between devices  14.7 us (15%)
  starting transfers between devices  12.9 us (13%)
  Pallas kernels  11.4 us (11%)
  local copies, waits for them, and re-layouts  3.04 us (3%)
    all_to_all x4, blocking collectives, exchange(): lax.all_to_all(values, axes, split_axis=0, concat_axis=0, axis_index_grou...  56.2 us
    all_to_all x1, waiting for transfers between devices, exchange(): lax.all_to_all(values, axes, split_axis=0, concat_axis=0, axis_index_grou...  12.4 us
    all_to_all x1, starting transfers between devices, exchange(): lax.all_to_all(values, axes, split_axis=0, concat_axis=0, axis_index_grou...  8.6 us
    pallas_call x1, Pallas kernels, body(): call(step_kernel, 'steps', (f32(FRAMES, COMP), f32(COMP * ROWS, WIDTH), f...  4.44 us
    ppermute x2, starting transfers between devices, swap(): lax.ppermute(values, 'frames', [(index, index ^ 1) for index in range(GRO...  4.33 us
    unnamed x10, local copies, waits for them, and re-layouts  3.04 us
    pallas_call x1, Pallas kernels, body(): call(register_kernel, 'register', f32(GROUP, LOCAL, ROWS, WIDTH), [HBM, H...  2.67 us
    ppermute x2, waiting for transfers between devices, swap(): lax.ppermute(values, 'frames', [(index, index ^ 1) for index in range(GRO...  2.32 us
  transfers between devices with their start and end apart: 3, of which 3 were waited for; matrix products, arithmetic and copies ran while one was open for 0% of the time, Pallas kernels for 2%

profile of v3, /device:TPU:1, one launch (start us, length us, event | category | flops | bytes accessed | tf_op | source)
XLA Modules:
  0.0 99.1 jit_solution(10376462200269142935)
XLA Ops:
  0.6 2.7 %register.1 = f32[32,8,8,128]{3,2,1,0:T(8,128)} custom-call(s32[2,8]{1,0:T(2,128)} %bitcast.25, f32[8,256,128]{2,1,0:T(8,128)} %bitcast.24), custom_call_target="tpu_custom_call" | custom-call | tf_op jit(solution)/shard_map/register/pallas_call | solution.py:235
  3.3 8.6 %all-to-all-start = ((f32[32,8,8,128]{3,2,1,0:T(8,128)}), f32[32,8,8,128]{3,2,1,0:T(8,128)S(1)}, u32[]{:S(2)}, u32[]{:S(2)}) async-start(f32[32,8,8,128]{3,2,1,0:T(8,128)} %register.1), calls=%async_computation | async-start | bytes 2097152 | tf_op jit(solution)/shard_map/all_to_all | solution.py:212
  11.9 0.1 pad_add_fusion.place_ref.core_ref
  12.0 0.0 copy-start.2
  12.0 1.2 %copy-done.2 = f32[256,1,1024]{2,1,0:T(1,128)S(1)} copy-done((f32[256,1,1024]{2,1,0:T(1,128)S(1)}, f32[256,1,1024]{2,1,0:T(1,128)}, u32[]{:S(2)}) %copy-start.2) | copy-done | bytes 1048600
  13.2 0.0 copy-start.3
  13.2 0.9 copy-done.3
  14.1 0.0 copy-start.4
  14.1 0.9 copy-done.4
  15.0 1.7 %spatial.1 = (f32[2048,128]{1,0:T(8,128)S(1)}, bf16[256,1024]{1,0:T(8,128)(2,1)S(1)}, bf16[256,1024]{1,0:T(8,128)(2,1)S(1)}, f32[256,128]{1,0:T(8,128)S(1)}, f32...) custom-call(s32[3]{0:T(128)S(1)} %pad_add_fusion.place_ref.core_ref, f32[2048,128]{1,0:T(8,128)S(1)} %bitcast.20, ...), custom_call_target="tpu_custom_call" | custom-call | flops 402653184 | bytes 4194304 | tf_op jit(solution)/shard_map/spatial/pallas_call | solution.py:249
  16.7 12.4 %all-to-all-done = f32[32,8,8,128]{3,2,1,0:T(8,128)S(1)} async-done(((f32[32,8,8,128]{3,2,1,0:T(8,128)}), f32[32,8,8,128]{3,2,1,0:T(8,128)S(1)}, u32[]{:S(2)}, u32[]{:S(2)}) %all-to-all-start) | async-done | bytes 1048608 | tf_op jit(solution)/shard_map/all_to_all | solution.py:212
  29.1 1.3 %cross.1 = (f32[128,512]{1,0:T(8,128)S(1)}, f32[128,512]{1,0:T(8,128)S(1)}, bf16[256,1024]{1,0:T(8,128)(2,1)S(1)}, bf16[256,1024]{1,0:T(8,128)(2,1)S(1)}) custom-call(s32[3]{0:T(128)S(1)} %pad_add_fusion.place_ref.core_ref, f32[2048,128]{1,0:T(8,128)S(1)} %bitcast.15, f32[8,128]{1,0:T(8,128)S(1)} %get-tuple-element.15.picture_ref, ...), custom_call_target="tpu_custom_call" | custom-call | tf_op jit(solution)/shard_map/cross/pallas_call | solution.py:256
  30.4 0.5 collective-permute-start
  30.9 1.2 %collective-permute-done.right_ref = f32[128,512]{1,0:T(8,128)S(1)} collective-permute-done((f32[128,512]{1,0:T(8,128)S(1)}, f32[128,512]{1,0:T(8,128)S(1)}, u32[]{:S(2)}, u32[]{:S(2)}) %collective-permute-start) | collective-permute-done | bytes 262176 | tf_op jit(solution)/shard_map/ppermute | solution.py:218
  32.1 11.4 %all_to_all.25.in_ref = f32[16,8,512]{2,1,0:T(8,128)S(1)} all-to-all(f32[16,8,512]{2,1,0:T(8,128)S(1)} %bitcast.16), channel_id=1, replica_groups={{0,16,32,48,64,80,96,112,128,144,160,176,192,208,224,240},{8,24,40,56,7..., dimensions={0} | all-to-all | bytes 524288 | tf_op jit(solution)/shard_map/all_to_all | solution.py:212
  43.6 15.9 %all_to_all.26.in_ref = f32[8,8,512]{2,1,0:T(8,128)S(1)} all-to-all(f32[8,8,512]{2,1,0:T(8,128)S(1)} %spread.2), channel_id=1, replica_groups=mesh['frames'=32,'planes'=8] {'planes'}, dimensions={0} | all-to-all | bytes 262144 | tf_op jit(solution)/shard_map/all_to_all | solution.py:212
  59.5 0.0 copy-start
  59.6 0.0 copy-start.1
  59.6 10.5 %all_to_all.27 = f32[16,8,512]{2,1,0:T(8,128)S(1)} all-to-all(f32[16,8,512]{2,1,0:T(8,128)S(1)} %spread.3), channel_id=1, replica_groups={{0,16,32,48,64,80,96,112,128,144,160,176,192,208,224,240},{8,24,40,56,7..., dimensions={0} | all-to-all | bytes 524288 | tf_op jit(solution)/shard_map/all_to_all | solution.py:212
  70.1 3.9 %collective-permute-start.1 = (f32[128,512]{1,0:T(8,128)S(1)}, f32[128,512]{1,0:T(8,128)S(1)}, u32[]{:S(2)}, u32[]{:S(2)}) collective-permute-start(f32[128,512]{1,0:T(8,128)S(1)} %bitcast.17), channel_id=1, source_target_pairs={{0,8},{8,0},{16,24},{24,16},{32,40},{40,32},{48,56},{56,48},{64,72... | collective-permute-start | bytes 786440 | tf_op jit(solution)/shard_map/ppermute | solution.py:218
  74.0 1.2 %collective-permute-done.1.other_ref = f32[128,512]{1,0:T(8,128)S(1)} collective-permute-done((f32[128,512]{1,0:T(8,128)S(1)}, f32[128,512]{1,0:T(8,128)S(1)}, u32[]{:S(2)}, u32[]{:S(2)}) %collective-permute-start.1) | collective-permute-done | bytes 262176 | tf_op jit(solution)/shard_map/ppermute | solution.py:218
  75.1 0.0 copy-done
  75.1 0.0 copy-done.1
  75.1 4.4 %steps.1 = (f32[256,256]{1,0:T(8,128)}, f32[2048,128]{1,0:T(8,128)S(1)}, f32[256,1,128]{2,1,0:T(1,128)S(1)}) custom-call(s32[3]{0:T(128)S(1)} %pad_add_fusion.place_ref.core_ref, f32[128,512]{1,0:T(8,128)S(1)} %bitcast.18, f32[128,512]{1,0:T(8,128)S(1)} %collective-permute-done.1.other_ref, f32[256,256]{1,0:T(8,128)S(1)} %copy-done, ...), custom_call_target="tpu_custom_call" | custom-call | tf_op jit(solution)/shard_map/steps/pallas_call | solution.py:271
  79.6 18.3 %all_to_all.28 = f32[256,1,128]{2,1,0:T(1,128)S(1)} all-to-all(f32[256,1,128]{2,1,0:T(1,128)S(1)} %get-tuple-element.25), channel_id=1, replica_groups=mesh['frames'=32,'planes'=8] {'frames','planes'}, dimensions={0} | all-to-all | bytes 262144 | tf_op jit(solution)/shard_map/all_to_all | solution.py:212
  97.8 1.2 %update.1 = f32[2048,128]{1,0:T(8,128)} custom-call(f32[32,8,128]{2,1,0:T(8,128)S(1)} %bitcast.19, f32[2048,128]{1,0:T(8,128)S(1)} %get-tuple-element.26.stack_ref, f32[2048,128]{1,0:T(8,128)S(1)} %get-tuple-element.27.grad_ref), custom_call_target="tpu_custom_call" | custom-call | tf_op jit(solution)/shard_map/update/pallas_call | solution.py:279
  (3 shorter events, 0.1 us)
Async XLA Ops:
  3.3 25.8 %all-to-all-start = ((f32[32,8,8,128]{3,2,1,0:T(8,128)}), f32[32,8,8,128]{3,2,1,0:T(8,128)S(1)}, u32[]{:S(2)}, u32[]{:S(2)}) async-start(f32[32,8,8,128]{3,2,1,0:T(8,128)} %register.1), calls=%async_computation | async-start | bytes 2097152 | tf_op jit(solution)/shard_map/all_to_all | solution.py:212
  12.0 1.2 %copy-start.2 = (f32[256,1,1024]{2,1,0:T(1,128)S(1)}, f32[256,1,1024]{2,1,0:T(1,128)}, u32[]{:S(2)}) copy-start(f32[256,1,1024]{2,1,0:T(1,128)} %param.12) | copy-start | bytes 3145732
  13.2 0.9 copy-start.3
  14.1 0.9 copy-start.4
  30.4 1.6 %collective-permute-start = (f32[128,512]{1,0:T(8,128)S(1)}, f32[128,512]{1,0:T(8,128)S(1)}, u32[]{:S(2)}, u32[]{:S(2)}) collective-permute-start(f32[128,512]{1,0:T(8,128)S(1)} %get-tuple-element.20), channel_id=1, source_target_pairs={{0,8},{8,0},{16,24},{24,16},{32,40},{40,32},{48,56},{56,48},{64,72... | collective-permute-start | bytes 786440 | tf_op jit(solution)/shard_map/ppermute | solution.py:218
  59.5 15.6 %copy-start = (f32[256,256]{1,0:T(8,128)S(1)}, f32[256,256]{1,0:T(8,128)}, u32[]{:S(2)}) copy-start(f32[256,256]{1,0:T(8,128)} %temporal_ref.1) | copy-start | bytes 786436
  59.6 15.6 %copy-start.1 = (f32[256,256]{1,0:T(8,128)S(1)}, f32[256,256]{1,0:T(8,128)}, u32[]{:S(2)}) copy-start(f32[256,256]{1,0:T(8,128)} %constant.13.clone.trend_ref) | copy-start | bytes 786436
  70.1 5.0 %collective-permute-start.1 = (f32[128,512]{1,0:T(8,128)S(1)}, f32[128,512]{1,0:T(8,128)S(1)}, u32[]{:S(2)}, u32[]{:S(2)}) collective-permute-start(f32[128,512]{1,0:T(8,128)S(1)} %bitcast.17), channel_id=1, source_target_pairs={{0,8},{8,0},{16,24},{24,16},{32,40},{40,32},{48,56},{56,48},{64,72... | collective-permute-start | bytes 786440 | tf_op jit(solution)/shard_map/ppermute | solution.py:218

commit v4 on v3

--- a/solution.py
+++ b/solution.py
@@ -43,10 +43,9 @@
 
 
 def dot(left, right, dims=NN):
-    def product(a, b):
-        return lax.dot_general(a, b, (dims, ((), ())), preferred_element_type=jnp.float32)
-
-    return product(left[0], right[0]) + (product(left[0], right[1]) + product(left[1], right[0]))
+    lefts = jnp.concatenate([left[0], left[0], left[1]], axis=1)
+    rights = jnp.concatenate([right[0], right[1], right[0]], axis=dims[1][0])
+    return lax.dot_general(lefts, rights, (dims, ((), ())), preferred_element_type=jnp.float32)
 
 
 def trend_projector():
@@ -88,7 +87,8 @@
 
 
 def spatial_kernel(place_ref, spatial_ref, support_ref, template_ref,
-                   stack_ref, high_ref, low_ref, mask_ref, pack_ref, picture_ref):
+                   stack_ref, high_ref, low_ref, mask_ref, pack_ref, picture_ref, upper_ref):
+    upper_ref[...] = jnp.broadcast_to(jnp.where(place_ref[2] == 0, 1.0, 0.0), upper_ref.shape)
     start = pl.multiple_of(place_ref[0] * ROWS, ROWS)
     picture_ref[...] = template_ref[pl.ds(start, ROWS), :]
     tile = place_ref[1] * GROUP + place_ref[0]
@@ -108,8 +108,8 @@
     pack_ref[HALF:, HALF:] = pltpu.roll(gram[:HALF, HALF:], HALF // 2, 1)
 
 
-def cross_kernel(core_ref, series_ref, picture_ref, spatial_high_ref, spatial_low_ref, gram_ref,
-                 keep_ref, give_ref, high_ref, low_ref, pack_ref):
+def cross_kernel(upper_ref, series_ref, picture_ref, spatial_high_ref, spatial_low_ref, gram_ref,
+                 keep_ref, give_ref, high_ref, low_ref):
     picture = picture_ref[...]
     numerator = jnp.zeros((FRAMES, WIDTH), jnp.float32)
     energy = jnp.zeros((FRAMES, WIDTH), jnp.float32)
@@ -122,15 +122,14 @@
     lane = lax.broadcasted_iota(jnp.int32, (FRAMES, 128), 1)
     extra = jnp.where(lane == HALF // 2, jnp.sum(numerator, axis=1, keepdims=True), jnp.sum(picture * picture))
     extra = jnp.where(lane == HALF // 2 + 1, jnp.sum(energy, axis=1, keepdims=True), extra)
-    pack_ref[:, :HALF] = gram_ref[:, :HALF]
-    pack_ref[:, HALF:2 * HALF] = jnp.where(lane < HALF // 2, gram_ref[:, HALF:], extra)
-    pack_ref[:, COMP:] = dot(
-        (high_ref[...], low_ref[...]), (spatial_high_ref[...], spatial_low_ref[...]), NT
-    )
-    mine = pl.multiple_of(core_ref[2] * HALF, HALF)
-    other = pl.multiple_of(HALF - core_ref[2] * HALF, HALF)
-    keep_ref[...] = pack_ref[pl.ds(mine, HALF), :]
-    give_ref[...] = pack_ref[pl.ds(other, HALF), :]
+    extra = jnp.where(lane < HALF // 2, gram_ref[:, HALF:], extra)
+    cross = dot((high_ref[...], low_ref[...]), (spatial_high_ref[...], spatial_low_ref[...]), NT)
+    upper = upper_ref[:1, :1] > 0.0
+    for columns, values in (
+        (slice(0, HALF), gram_ref[:, :HALF]), (slice(HALF, COMP), extra), (slice(COMP, PACK), cross)
+    ):
+        give_ref[:, columns] = jnp.where(upper, values[HALF:], values[:HALF])
+        keep_ref[:, columns] = jnp.where(upper, values[:HALF], values[HALF:])
 
 
 def add_kernel(left_ref, right_ref, out_ref):
@@ -142,29 +141,27 @@
     out_ref[...] = jnp.broadcast_to(total[None], out_ref.shape)
 
 
-def step_kernel(core_ref, mine_ref, other_ref, temporal_ref, trend_ref, mask_ref,
+def step_kernel(upper_ref, mine_ref, other_ref, temporal_ref, trend_ref, mask_ref,
                 spatial_high_ref, spatial_low_ref, high_ref, low_ref,
-                out_ref, grad_ref, sums_ref, pack_ref):
-    mine = pl.multiple_of(core_ref[2] * HALF, HALF)
-    other = pl.multiple_of(HALF - core_ref[2] * HALF, HALF)
-    pack_ref[pl.ds(mine, HALF), :] = mine_ref[...]
-    pack_ref[pl.ds(other, HALF), :] = other_ref[...]
+                out_ref, grad_ref, sums_ref):
+    first = upper_ref[:1, :1] > 0.0
+    upper = jnp.where(first, mine_ref[...], other_ref[...])
+    lower = jnp.where(first, other_ref[...], mine_ref[...])
     lane = lax.broadcasted_iota(jnp.int32, (HALF, HALF), 1)
     corner = jnp.where(
-        lane < HALF // 2,
-        pack_ref[:HALF, HALF:2 * HALF],
-        pltpu.roll(pack_ref[HALF:, HALF:2 * HALF], HALF // 2, 1),
+        lane < HALF // 2, upper[:, HALF:2 * HALF], pltpu.roll(lower[:, HALF:2 * HALF], HALF // 2, 1)
     )
     gram = split(jnp.concatenate([
-        jnp.concatenate([pack_ref[:HALF, :HALF], corner], axis=1),
-        jnp.concatenate([jnp.transpose(corner), pack_ref[HALF:, :HALF]], axis=1),
+        jnp.concatenate([upper[:, :HALF], corner], axis=1),
+        jnp.concatenate([jnp.transpose(corner), lower[:, :HALF]], axis=1),
     ], axis=0))
-    extra = pack_ref[:, HALF:2 * HALF]
+    pack = jnp.concatenate([upper, lower], axis=0)
+    extra = pack[:, HALF:2 * HALF]
     first = HALF // 2
     energy = extra[:, first + 1:first + 2] * extra[:, first + 2:first + 3]
     weight = extra[:, first:first + 1] / jnp.sqrt(energy + epsilon)
     trend = split(trend_ref[...])
-    cross = pack_ref[:, COMP:] * weight
+    cross = pack[:, COMP:] * weight
     cross = cross - dot(trend, split(cross))
     temporal = temporal_ref[...]
     grad = dot(split(temporal), gram) - cross
@@ -246,19 +243,18 @@
     )(shift_table, movie)
     series = exchange(payload, "frames").reshape(FRAMES * ROWS, WIDTH)
     spatial = spatial_init.reshape(COMP * ROWS, WIDTH)
-    stack, spatial_high, spatial_low, mask, gram, picture = call(
+    stack, spatial_high, spatial_low, mask, gram, picture, upper = call(
         spatial_kernel, "spatial",
         (f32(COMP * ROWS, WIDTH), b16(COMP, TILE), b16(COMP, TILE), f32(COMP, 128), f32(COMP, COMP),
-         f32(ROWS, WIDTH)),
+         f32(ROWS, WIDTH), f32(8, 128)),
         [SMEM] + [VMEM] * 3,
         cost=pl.CostEstimate(flops=6 * COMP * COMP * TILE, bytes_accessed=4 << 20, transcendentals=0),
     )(place, spatial, support.T, template.reshape(HEIGHT, WIDTH))
     keep, give, high, low = call(
         cross_kernel, "cross",
         (f32(HALF, PACK), f32(HALF, PACK), b16(FRAMES, TILE), b16(FRAMES, TILE)),
-        [SMEM] + [VMEM] * 5,
-        scratch_shapes=[pltpu.VMEM((FRAMES, PACK), jnp.float32)],
-    )(place, series, picture, spatial_high, spatial_low, gram)
+        [VMEM] * 6,
+    )(upper, series, picture, spatial_high, spatial_low, gram)
 
     def spread(values, copies):
         return call(spread_kernel, "spread", f32(copies, *values.shape[1:]), [VMEM])(values)
@@ -271,9 +267,8 @@
     temporal, grad, sums = call(
         step_kernel, "steps",
         (f32(FRAMES, COMP), f32(COMP * ROWS, WIDTH), f32(GROUP * PLANES, 1, 128)),
-        [SMEM] + [VMEM] * 9,
-        scratch_shapes=[pltpu.VMEM((FRAMES, PACK), jnp.float32)],
-    )(place, mine, swap(mine), temporal_init, jnp.asarray(trend_projector()), mask,
+        [VMEM] * 10,
+    )(upper, mine, swap(mine), temporal_init, jnp.asarray(trend_projector()), mask,
       spatial_high, spatial_low, high, low)
     sums = exchange(sums, ("frames", "planes")).reshape(GROUP, PLANES, 128)
     spatial = call(

time: 99.5 us -> 98 us (0.985)
  Pallas kernels: 11.4 us -> 9.89 us
where the time goes in v4:
time: 98 us; the launch traced here: 97.6 us
  blocking collectives  56.2 us (57%)
  waiting for transfers between devices  14.8 us (15%)
  starting transfers between devices  12.9 us (13%)
  Pallas kernels  9.89 us (10%)
  local copies, waits for them, and re-layouts  3.04 us (3%)
    all_to_all x4, blocking collectives, exchange(): lax.all_to_all(values, axes, split_axis=0, concat_axis=0, axis_index_grou...  56.2 us
    all_to_all x1, waiting for transfers between devices, exchange(): lax.all_to_all(values, axes, split_axis=0, concat_axis=0, axis_index_grou...  12.4 us
    all_to_all x1, starting transfers between devices, exchange(): lax.all_to_all(values, axes, split_axis=0, concat_axis=0, axis_index_grou...  8.59 us
    ppermute x2, starting transfers between devices, swap(): lax.ppermute(values, 'frames', [(index, index ^ 1) for index in range(GRO...  4.33 us
    pallas_call x1, Pallas kernels, body(): call(step_kernel, 'steps', (f32(FRAMES, COMP), f32(COMP * ROWS, WIDTH), f...  3.48 us
    unnamed x10, local copies, waits for them, and re-layouts  3.04 us
    pallas_call x1, Pallas kernels, body(): call(register_kernel, 'register', f32(GROUP, LOCAL, ROWS, WIDTH), [HBM, H...  2.66 us
    ppermute x2, waiting for transfers between devices, swap(): lax.ppermute(values, 'frames', [(index, index ^ 1) for index in range(GRO...  2.32 us
  transfers between devices with their start and end apart: 3, of which 3 were waited for; matrix products, arithmetic and copies ran while one was open for 0% of the time, Pallas kernels for 2%

profile of v4, /device:TPU:1, one launch (start us, length us, event | category | flops | bytes accessed | tf_op | source)
XLA Modules:
  0.0 97.6 jit_solution(3100952632898491050)
XLA Ops:
  0.6 2.7 %register.1 = f32[32,8,8,128]{3,2,1,0:T(8,128)} custom-call(s32[2,8]{1,0:T(2,128)} %bitcast.25, f32[8,256,128]{2,1,0:T(8,128)} %bitcast.24), custom_call_target="tpu_custom_call" | custom-call | tf_op jit(solution)/shard_map/register/pallas_call | solution.py:232
  3.3 8.6 %all-to-all-start = ((f32[32,8,8,128]{3,2,1,0:T(8,128)}), f32[32,8,8,128]{3,2,1,0:T(8,128)S(1)}, u32[]{:S(2)}, u32[]{:S(2)}) async-start(f32[32,8,8,128]{3,2,1,0:T(8,128)} %register.1), calls=%async_computation | async-start | bytes 2097152 | tf_op jit(solution)/shard_map/all_to_all | solution.py:209
  11.9 0.1 pad_add_fusion.place_ref
  12.0 0.0 copy-start.2
  12.0 1.2 %copy-done.2 = f32[256,1,1024]{2,1,0:T(1,128)S(1)} copy-done((f32[256,1,1024]{2,1,0:T(1,128)S(1)}, f32[256,1,1024]{2,1,0:T(1,128)}, u32[]{:S(2)}) %copy-start.2) | copy-done | bytes 1048600
  13.2 0.0 copy-start.3
  13.2 0.9 copy-done.3
  14.1 0.0 copy-start.4
  14.1 0.9 copy-done.4
  15.0 1.6 %spatial.1 = (f32[2048,128]{1,0:T(8,128)S(1)}, bf16[256,1024]{1,0:T(8,128)(2,1)S(1)}, bf16[256,1024]{1,0:T(8,128)(2,1)S(1)}, f32[256,128]{1,0:T(8,128)S(1)}, f32...) custom-call(s32[3]{0:T(128)S(1)} %pad_add_fusion.place_ref, f32[2048,128]{1,0:T(8,128)S(1)} %bitcast.20, ...), custom_call_target="tpu_custom_call" | custom-call | flops 402653184 | bytes 4194304 | tf_op jit(solution)/shard_map/spatial/pallas_call | solution.py:246
  16.6 12.4 %all-to-all-done = f32[32,8,8,128]{3,2,1,0:T(8,128)S(1)} async-done(((f32[32,8,8,128]{3,2,1,0:T(8,128)}), f32[32,8,8,128]{3,2,1,0:T(8,128)S(1)}, u32[]{:S(2)}, u32[]{:S(2)}) %all-to-all-start) | async-done | bytes 1048608 | tf_op jit(solution)/shard_map/all_to_all | solution.py:209
  29.1 0.8 cross.1
  29.9 0.5 collective-permute-start
  30.4 1.2 %collective-permute-done.right_ref = f32[128,512]{1,0:T(8,128)S(1)} collective-permute-done((f32[128,512]{1,0:T(8,128)S(1)}, f32[128,512]{1,0:T(8,128)S(1)}, u32[]{:S(2)}, u32[]{:S(2)}) %collective-permute-start) | collective-permute-done | bytes 262176 | tf_op jit(solution)/shard_map/ppermute | solution.py:215
  31.6 11.4 %all_to_all.25.in_ref = f32[16,8,512]{2,1,0:T(8,128)S(1)} all-to-all(f32[16,8,512]{2,1,0:T(8,128)S(1)} %bitcast.18), channel_id=1, replica_groups={{0,16,32,48,64,80,96,112,128,144,160,176,192,208,224,240},{8,24,40,56,7..., dimensions={0} | all-to-all | bytes 524288 | tf_op jit(solution)/shard_map/all_to_all | solution.py:209
  43.0 15.9 %all_to_all.26.in_ref = f32[8,8,512]{2,1,0:T(8,128)S(1)} all-to-all(f32[8,8,512]{2,1,0:T(8,128)S(1)} %spread.2), channel_id=1, replica_groups=mesh['frames'=32,'planes'=8] {'planes'}, dimensions={0} | all-to-all | bytes 262144 | tf_op jit(solution)/shard_map/all_to_all | solution.py:209
  59.0 0.0 copy-start
  59.0 0.0 copy-start.1
  59.0 10.5 %all_to_all.27 = f32[16,8,512]{2,1,0:T(8,128)S(1)} all-to-all(f32[16,8,512]{2,1,0:T(8,128)S(1)} %spread.3), channel_id=1, replica_groups={{0,16,32,48,64,80,96,112,128,144,160,176,192,208,224,240},{8,24,40,56,7..., dimensions={0} | all-to-all | bytes 524288 | tf_op jit(solution)/shard_map/all_to_all | solution.py:209
  69.5 3.9 %collective-permute-start.1 = (f32[128,512]{1,0:T(8,128)S(1)}, f32[128,512]{1,0:T(8,128)S(1)}, u32[]{:S(2)}, u32[]{:S(2)}) collective-permute-start(f32[128,512]{1,0:T(8,128)S(1)} %bitcast.16), channel_id=1, source_target_pairs={{0,8},{8,0},{16,24},{24,16},{32,40},{40,32},{48,56},{56,48},{64,72... | collective-permute-start | bytes 786440 | tf_op jit(solution)/shard_map/ppermute | solution.py:215
  73.4 1.2 %collective-permute-done.1.other_ref = f32[128,512]{1,0:T(8,128)S(1)} collective-permute-done((f32[128,512]{1,0:T(8,128)S(1)}, f32[128,512]{1,0:T(8,128)S(1)}, u32[]{:S(2)}, u32[]{:S(2)}) %collective-permute-start.1) | collective-permute-done | bytes 262176 | tf_op jit(solution)/shard_map/ppermute | solution.py:215
  74.6 0.0 copy-done
  74.6 0.0 copy-done.1
  74.6 3.5 %steps.1 = (f32[256,256]{1,0:T(8,128)}, f32[2048,128]{1,0:T(8,128)S(1)}, f32[256,1,128]{2,1,0:T(1,128)S(1)}) custom-call(f32[8,128]{1,0:T(8,128)S(1)} %get-tuple-element.16.upper_ref, f32[128,512]{1,0:T(8,128)S(1)} %bitcast.17, f32[128,512]{1,0:T(8,128)S(1)} %collective-permute-done.1.other_ref, f32[256,256]{1,0:T(8,128)S(1)} %copy-done, ...), custom_call_target="tpu_custom_call" | custom-call | tf_op jit(solution)/shard_map/steps/pallas_call | solution.py:267
  78.0 18.3 %all_to_all.28 = f32[256,1,128]{2,1,0:T(1,128)S(1)} all-to-all(f32[256,1,128]{2,1,0:T(1,128)S(1)} %get-tuple-element.27), channel_id=1, replica_groups=mesh['frames'=32,'planes'=8] {'frames','planes'}, dimensions={0} | all-to-all | bytes 262144 | tf_op jit(solution)/shard_map/all_to_all | solution.py:209
  96.3 1.2 %update.1 = f32[2048,128]{1,0:T(8,128)} custom-call(f32[32,8,128]{2,1,0:T(8,128)S(1)} %bitcast.19, f32[2048,128]{1,0:T(8,128)S(1)} %get-tuple-element.28.stack_ref, f32[2048,128]{1,0:T(8,128)S(1)} %get-tuple-element.29.grad_ref), custom_call_target="tpu_custom_call" | custom-call | tf_op jit(solution)/shard_map/update/pallas_call | solution.py:274
  (3 shorter events, 0.1 us)
Async XLA Ops:
  3.3 25.8 %all-to-all-start = ((f32[32,8,8,128]{3,2,1,0:T(8,128)}), f32[32,8,8,128]{3,2,1,0:T(8,128)S(1)}, u32[]{:S(2)}, u32[]{:S(2)}) async-start(f32[32,8,8,128]{3,2,1,0:T(8,128)} %register.1), calls=%async_computation | async-start | bytes 2097152 | tf_op jit(solution)/shard_map/all_to_all | solution.py:209
  12.0 1.2 %copy-start.2 = (f32[256,1,1024]{2,1,0:T(1,128)S(1)}, f32[256,1,1024]{2,1,0:T(1,128)}, u32[]{:S(2)}) copy-start(f32[256,1,1024]{2,1,0:T(1,128)} %param.12) | copy-start | bytes 3145732
  13.2 0.9 copy-start.3
  14.1 0.9 copy-start.4
  29.9 1.6 %collective-permute-start = (f32[128,512]{1,0:T(8,128)S(1)}, f32[128,512]{1,0:T(8,128)S(1)}, u32[]{:S(2)}, u32[]{:S(2)}) collective-permute-start(f32[128,512]{1,0:T(8,128)S(1)} %get-tuple-element.22), channel_id=1, source_target_pairs={{0,8},{8,0},{16,24},{24,16},{32,40},{40,32},{48,56},{56,48},{64,72... | collective-permute-start | bytes 786440 | tf_op jit(solution)/shard_map/ppermute | solution.py:215
  59.0 15.6 %copy-start = (f32[256,256]{1,0:T(8,128)S(1)}, f32[256,256]{1,0:T(8,128)}, u32[]{:S(2)}) copy-start(f32[256,256]{1,0:T(8,128)} %temporal_ref.1) | copy-start | bytes 786436
  59.0 15.6 %copy-start.1 = (f32[256,256]{1,0:T(8,128)S(1)}, f32[256,256]{1,0:T(8,128)}, u32[]{:S(2)}) copy-start(f32[256,256]{1,0:T(8,128)} %constant.13.clone.trend_ref) | copy-start | bytes 786436
  69.5 5.0 %collective-permute-start.1 = (f32[128,512]{1,0:T(8,128)S(1)}, f32[128,512]{1,0:T(8,128)S(1)}, u32[]{:S(2)}, u32[]{:S(2)}) collective-permute-start(f32[128,512]{1,0:T(8,128)S(1)} %bitcast.16), channel_id=1, source_target_pairs={{0,8},{8,0},{16,24},{24,16},{32,40},{40,32},{48,56},{56,48},{64,72... | collective-permute-start | bytes 786440 | tf_op jit(solution)/shard_map/ppermute | solution.py:215

commit v5 on v4

--- a/solution.py
+++ b/solution.py
@@ -19,6 +19,8 @@
 PACK = 512
 HALF = 128
 MAXS = 16
+BATCH = 4
+BLOCKS = 8
 epsilon = 1e-06
 
 VMEM = pl.BlockSpec(memory_space=pltpu.VMEM)
@@ -68,20 +70,23 @@
         copy.start()
     table.wait()
     stores = []
-    for frame in range(LOCAL):
-        copies[frame].wait()
-        right = jnp.mod(shift_ref[1, frame], WIDTH)
-        picture = pltpu.roll(movie_ref[frame], right, 1)
-        wide = wide_ref.at[frame]
-        wide[pl.ds(0, MAXS), :] = picture[HEIGHT - MAXS:]
-        wide[pl.ds(MAXS, HEIGHT), :] = picture
-        wide[pl.ds(MAXS + HEIGHT, MAXS), :] = picture[:MAXS]
-        moved = wide[pl.ds(MAXS - shift_ref[0, frame], HEIGHT), :]
-        moved_ref[frame] = moved.reshape(GROUP, ROWS, WIDTH)
-        stores.append(
-            pltpu.make_async_copy(moved_ref.at[frame], out_hbm.at[:, frame], moved_sem.at[frame])
-        )
-        stores[frame].start()
+    for start in range(0, LOCAL, BATCH):
+        frames = range(start, start + BATCH)
+        for frame in frames:
+            copies[frame].wait()
+        for frame in frames:
+            picture = pltpu.roll(movie_ref[frame], jnp.mod(shift_ref[1, frame], WIDTH), 1)
+            wide = wide_ref.at[frame]
+            wide[pl.ds(0, MAXS), :] = picture[HEIGHT - MAXS:]
+            wide[pl.ds(MAXS, HEIGHT), :] = picture
+            wide[pl.ds(MAXS + HEIGHT, MAXS), :] = picture[:MAXS]
+        for frame in frames:
+            moved = wide_ref[frame, pl.ds(MAXS - shift_ref[0, frame], HEIGHT), :]
+            moved_ref[frame] = moved.reshape(GROUP, ROWS, WIDTH)
+        for frame in frames:
+            store = pltpu.make_async_copy(moved_ref.at[frame], out_hbm.at[:, frame], moved_sem.at[frame])
+            store.start()
+            stores.append(store)
     for store in stores:
         store.wait()
 
@@ -141,6 +146,16 @@
     out_ref[...] = jnp.broadcast_to(total[None], out_ref.shape)
 
 
+def weigh_kernel(in_ref, out_ref):
+    total = jnp.sum(in_ref[...], axis=0)
+    first = HALF + HALF // 2
+    energy = total[:, first + 1:first + 2] * total[:, first + 2:first + 3]
+    weight = total[:, first:first + 1] / jnp.sqrt(energy + epsilon)
+    column = lax.broadcasted_iota(jnp.int32, (LOCAL, PACK), 1)
+    total = jnp.where(column >= COMP, total * weight, jnp.where(column == first, weight, total))
+    out_ref[...] = jnp.broadcast_to(total[None], out_ref.shape)
+
+
 def step_kernel(upper_ref, mine_ref, other_ref, temporal_ref, trend_ref, mask_ref,
                 spatial_high_ref, spatial_low_ref, high_ref, low_ref,
                 out_ref, grad_ref, sums_ref):
@@ -156,15 +171,11 @@
         jnp.concatenate([jnp.transpose(corner), lower[:, :HALF]], axis=1),
     ], axis=0))
     pack = jnp.concatenate([upper, lower], axis=0)
-    extra = pack[:, HALF:2 * HALF]
-    first = HALF // 2
-    energy = extra[:, first + 1:first + 2] * extra[:, first + 2:first + 3]
-    weight = extra[:, first:first + 1] / jnp.sqrt(energy + epsilon)
+    weight = pack[:, HALF + HALF // 2:HALF + HALF // 2 + 1]
+    cross = pack[:, COMP:]
     trend = split(trend_ref[...])
-    cross = pack[:, COMP:] * weight
-    cross = cross - dot(trend, split(cross))
     temporal = temporal_ref[...]
-    grad = dot(split(temporal), gram) - cross
+    grad = dot(split(temporal), gram) + dot(trend, split(cross)) - cross
     step = jnp.sum(grad * grad) / (jnp.sum(grad * dot(split(grad), gram)) + epsilon)
     temporal = jnp.maximum(temporal - step * grad, 0.0)
     out_ref[...] = temporal
@@ -185,14 +196,11 @@
     sums_ref[...] = jnp.where(lane == 0, square, jnp.where(lane == 1, curve, 0.0))
 
 
-BLOCKS = 4
-
-
 def final_kernel(sums_ref, stack_ref, grad_ref, out_hbm, out_ref, sems):
     totals = jnp.sum(jnp.sum(sums_ref[...], axis=0), axis=0, keepdims=True)
     lane = lax.broadcasted_iota(jnp.int32, totals.shape, 1)
-    square = jnp.sum(jnp.where(lane == 0, totals, 0.0))
-    curve = jnp.sum(jnp.where(lane == 1, totals, 0.0))
+    square = jnp.sum(jnp.where(lane == 0, totals, 0.0), axis=1, keepdims=True)
+    curve = jnp.sum(jnp.where(lane == 1, totals, 0.0), axis=1, keepdims=True)
     step = square / (curve + epsilon)
     size = COMP * ROWS // BLOCKS
     stores = []
@@ -256,14 +264,14 @@
         [VMEM] * 6,
     )(upper, series, picture, spatial_high, spatial_low, gram)
 
-    def spread(values, copies):
-        return call(spread_kernel, "spread", f32(copies, *values.shape[1:]), [VMEM])(values)
+    def spread(kernel, name, values, copies):
+        return call(kernel, name, f32(copies, *values.shape[1:]), [VMEM])(values)
 
     chips = [list(range(core, GROUP, 2)) for core in range(2)]
     part = call(add_kernel, "pair", f32(HALF, PACK), [VMEM] * 2)(keep, swap(give))
     part = exchange(part.reshape(GROUP // 2, LOCAL, PACK), "frames", chips)
-    part = exchange(spread(part, PLANES), "planes")
-    mine = exchange(spread(part, GROUP // 2), "frames", chips).reshape(HALF, PACK)
+    part = exchange(spread(spread_kernel, "spread", part, PLANES), "planes")
+    mine = exchange(spread(weigh_kernel, "weigh", part, GROUP // 2), "frames", chips).reshape(HALF, PACK)
     temporal, grad, sums = call(
         step_kernel, "steps",
         (f32(FRAMES, COMP), f32(COMP * ROWS, WIDTH), f32(GROUP * PLANES, 1, 128)),

time: 98 us -> 97.8 us (level)
  no operation moved by 1% of the time
where the time goes in v5:
time: 97.8 us; the launch traced here: 97.4 us
  blocking collectives  56.2 us (57%)
  waiting for transfers between devices  14.8 us (15%)
  starting transfers between devices  12.9 us (13%)
  Pallas kernels  9.68 us (10%)
  local copies, waits for them, and re-layouts  3.04 us (3%)
    all_to_all x4, blocking collectives, exchange(): lax.all_to_all(values, axes, split_axis=0, concat_axis=0, axis_index_grou...  56.2 us
    all_to_all x1, waiting for transfers between devices, exchange(): lax.all_to_all(values, axes, split_axis=0, concat_axis=0, axis_index_grou...  12.4 us
    all_to_all x1, starting transfers between devices, exchange(): lax.all_to_all(values, axes, split_axis=0, concat_axis=0, axis_index_grou...  8.6 us
    ppermute x2, starting transfers between devices, swap(): lax.ppermute(values, 'frames', [(index, index ^ 1) for index in range(GRO...  4.33 us
    pallas_call x1, Pallas kernels, body(): call(step_kernel, 'steps', (f32(FRAMES, COMP), f32(COMP * ROWS, WIDTH), f...  3.27 us
    unnamed x10, local copies, waits for them, and re-layouts  3.04 us
    pallas_call x1, Pallas kernels, body(): call(register_kernel, 'register', f32(GROUP, LOCAL, ROWS, WIDTH), [HBM, H...  2.52 us
    ppermute x2, waiting for transfers between devices, swap(): lax.ppermute(values, 'frames', [(index, index ^ 1) for index in range(GRO...  2.32 us
  transfers between devices with their start and end apart: 3, of which 3 were waited for; matrix products, arithmetic and copies ran while one was open for 0% of the time, Pallas kernels for 2%

profile of v5, /device:TPU:1, one launch (start us, length us, event | category | flops | bytes accessed | tf_op | source)
XLA Modules:
  0.0 97.4 jit_solution(4734119784216443885)
XLA Ops:
  0.6 2.5 %register.1 = f32[32,8,8,128]{3,2,1,0:T(8,128)} custom-call(s32[2,8]{1,0:T(2,128)} %bitcast.25, f32[8,256,128]{2,1,0:T(8,128)} %bitcast.24), custom_call_target="tpu_custom_call" | custom-call | tf_op jit(solution)/shard_map/register/pallas_call | solution.py:240
  3.2 8.6 %all-to-all-start = ((f32[32,8,8,128]{3,2,1,0:T(8,128)}), f32[32,8,8,128]{3,2,1,0:T(8,128)S(1)}, u32[]{:S(2)}, u32[]{:S(2)}) async-start(f32[32,8,8,128]{3,2,1,0:T(8,128)} %register.1), calls=%async_computation | async-start | bytes 2097152 | tf_op jit(solution)/shard_map/all_to_all | solution.py:217
  11.8 0.1 pad_add_fusion.place_ref
  11.8 0.0 copy-start.2
  11.8 1.2 %copy-done.2 = f32[256,1,1024]{2,1,0:T(1,128)S(1)} copy-done((f32[256,1,1024]{2,1,0:T(1,128)S(1)}, f32[256,1,1024]{2,1,0:T(1,128)}, u32[]{:S(2)}) %copy-start.2) | copy-done | bytes 1048600
  13.1 0.0 copy-start.3
  13.1 0.9 copy-done.3
  14.0 0.0 copy-start.4
  14.0 0.9 copy-done.4
  14.9 1.6 %spatial.1 = (f32[2048,128]{1,0:T(8,128)S(1)}, bf16[256,1024]{1,0:T(8,128)(2,1)S(1)}, bf16[256,1024]{1,0:T(8,128)(2,1)S(1)}, f32[256,128]{1,0:T(8,128)S(1)}, f32...) custom-call(s32[3]{0:T(128)S(1)} %pad_add_fusion.place_ref, f32[2048,128]{1,0:T(8,128)S(1)} %bitcast.20, ...), custom_call_target="tpu_custom_call" | custom-call | flops 402653184 | bytes 4194304 | tf_op jit(solution)/shard_map/spatial/pallas_call | solution.py:254
  16.5 12.4 %all-to-all-done = f32[32,8,8,128]{3,2,1,0:T(8,128)S(1)} async-done(((f32[32,8,8,128]{3,2,1,0:T(8,128)}), f32[32,8,8,128]{3,2,1,0:T(8,128)S(1)}, u32[]{:S(2)}, u32[]{:S(2)}) %all-to-all-start) | async-done | bytes 1048608 | tf_op jit(solution)/shard_map/all_to_all | solution.py:217
  28.9 0.8 cross.1
  29.7 0.5 collective-permute-start
  30.2 1.2 %collective-permute-done.right_ref = f32[128,512]{1,0:T(8,128)S(1)} collective-permute-done((f32[128,512]{1,0:T(8,128)S(1)}, f32[128,512]{1,0:T(8,128)S(1)}, u32[]{:S(2)}, u32[]{:S(2)}) %collective-permute-start) | collective-permute-done | bytes 262176 | tf_op jit(solution)/shard_map/ppermute | solution.py:223
  31.4 11.4 %all_to_all.25.in_ref = f32[16,8,512]{2,1,0:T(8,128)S(1)} all-to-all(f32[16,8,512]{2,1,0:T(8,128)S(1)} %bitcast.18), channel_id=1, replica_groups={{0,16,32,48,64,80,96,112,128,144,160,176,192,208,224,240},{8,24,40,56,7..., dimensions={0} | all-to-all | bytes 524288 | tf_op jit(solution)/shard_map/all_to_all | solution.py:217
  42.9 15.9 %all_to_all.26.in_ref = f32[8,8,512]{2,1,0:T(8,128)S(1)} all-to-all(f32[8,8,512]{2,1,0:T(8,128)S(1)} %spread.1), channel_id=1, replica_groups=mesh['frames'=32,'planes'=8] {'planes'}, dimensions={0} | all-to-all | bytes 262144 | tf_op jit(solution)/shard_map/all_to_all | solution.py:217
  58.8 0.2 weigh.1
  59.1 0.0 copy-start
  59.1 0.0 copy-start.1
  59.1 10.5 %all_to_all.27 = f32[16,8,512]{2,1,0:T(8,128)S(1)} all-to-all(f32[16,8,512]{2,1,0:T(8,128)S(1)} %weigh.1), channel_id=1, replica_groups={{0,16,32,48,64,80,96,112,128,144,160,176,192,208,224,240},{8,24,40,56,7..., dimensions={0} | all-to-all | bytes 524288 | tf_op jit(solution)/shard_map/all_to_all | solution.py:217
  69.6 3.9 %collective-permute-start.1 = (f32[128,512]{1,0:T(8,128)S(1)}, f32[128,512]{1,0:T(8,128)S(1)}, u32[]{:S(2)}, u32[]{:S(2)}) collective-permute-start(f32[128,512]{1,0:T(8,128)S(1)} %bitcast.16), channel_id=1, source_target_pairs={{0,8},{8,0},{16,24},{24,16},{32,40},{40,32},{48,56},{56,48},{64,72... | collective-permute-start | bytes 786440 | tf_op jit(solution)/shard_map/ppermute | solution.py:223
  73.5 1.2 %collective-permute-done.1.other_ref = f32[128,512]{1,0:T(8,128)S(1)} collective-permute-done((f32[128,512]{1,0:T(8,128)S(1)}, f32[128,512]{1,0:T(8,128)S(1)}, u32[]{:S(2)}, u32[]{:S(2)}) %collective-permute-start.1) | collective-permute-done | bytes 262176 | tf_op jit(solution)/shard_map/ppermute | solution.py:223
  74.6 0.0 copy-done
  74.6 0.0 copy-done.1
  74.6 3.3 %steps.1 = (f32[256,256]{1,0:T(8,128)}, f32[2048,128]{1,0:T(8,128)S(1)}, f32[256,1,128]{2,1,0:T(1,128)S(1)}) custom-call(f32[8,128]{1,0:T(8,128)S(1)} %get-tuple-element.16.upper_ref, f32[128,512]{1,0:T(8,128)S(1)} %bitcast.17, f32[128,512]{1,0:T(8,128)S(1)} %collective-permute-done.1.other_ref, f32[256,256]{1,0:T(8,128)S(1)} %copy-done, ...), custom_call_target="tpu_custom_call" | custom-call | tf_op jit(solution)/shard_map/steps/pallas_call | solution.py:275
  77.9 18.3 %all_to_all.28 = f32[256,1,128]{2,1,0:T(1,128)S(1)} all-to-all(f32[256,1,128]{2,1,0:T(1,128)S(1)} %get-tuple-element.27), channel_id=1, replica_groups=mesh['frames'=32,'planes'=8] {'frames','planes'}, dimensions={0} | all-to-all | bytes 262144 | tf_op jit(solution)/shard_map/all_to_all | solution.py:217
  96.2 1.2 %update.1 = f32[2048,128]{1,0:T(8,128)} custom-call(f32[32,8,128]{2,1,0:T(8,128)S(1)} %bitcast.19, f32[2048,128]{1,0:T(8,128)S(1)} %get-tuple-element.28.stack_ref, f32[2048,128]{1,0:T(8,128)S(1)} %get-tuple-element.29.grad_ref), custom_call_target="tpu_custom_call" | custom-call | tf_op jit(solution)/shard_map/update/pallas_call | solution.py:282
  (2 shorter events, 0.1 us)
Async XLA Ops:
  3.2 25.8 %all-to-all-start = ((f32[32,8,8,128]{3,2,1,0:T(8,128)}), f32[32,8,8,128]{3,2,1,0:T(8,128)S(1)}, u32[]{:S(2)}, u32[]{:S(2)}) async-start(f32[32,8,8,128]{3,2,1,0:T(8,128)} %register.1), calls=%async_computation | async-start | bytes 2097152 | tf_op jit(solution)/shard_map/all_to_all | solution.py:217
  11.8 1.2 %copy-start.2 = (f32[256,1,1024]{2,1,0:T(1,128)S(1)}, f32[256,1,1024]{2,1,0:T(1,128)}, u32[]{:S(2)}) copy-start(f32[256,1,1024]{2,1,0:T(1,128)} %param.12) | copy-start | bytes 3145732
  13.1 0.9 copy-start.3
  14.0 0.9 copy-start.4
  29.7 1.6 %collective-permute-start = (f32[128,512]{1,0:T(8,128)S(1)}, f32[128,512]{1,0:T(8,128)S(1)}, u32[]{:S(2)}, u32[]{:S(2)}) collective-permute-start(f32[128,512]{1,0:T(8,128)S(1)} %get-tuple-element.22), channel_id=1, source_target_pairs={{0,8},{8,0},{16,24},{24,16},{32,40},{40,32},{48,56},{56,48},{64,72... | collective-permute-start | bytes 786440 | tf_op jit(solution)/shard_map/ppermute | solution.py:223
  59.1 15.6 %copy-start = (f32[256,256]{1,0:T(8,128)S(1)}, f32[256,256]{1,0:T(8,128)}, u32[]{:S(2)}) copy-start(f32[256,256]{1,0:T(8,128)} %temporal_ref.1) | copy-start | bytes 786436
  59.1 15.6 %copy-start.1 = (f32[256,256]{1,0:T(8,128)S(1)}, f32[256,256]{1,0:T(8,128)}, u32[]{:S(2)}) copy-start(f32[256,256]{1,0:T(8,128)} %constant.13.clone.trend_ref) | copy-start | bytes 786436
  69.6 5.0 %collective-permute-start.1 = (f32[128,512]{1,0:T(8,128)S(1)}, f32[128,512]{1,0:T(8,128)S(1)}, u32[]{:S(2)}, u32[]{:S(2)}) collective-permute-start(f32[128,512]{1,0:T(8,128)S(1)} %bitcast.16), channel_id=1, source_target_pairs={{0,8},{8,0},{16,24},{24,16},{32,40},{40,32},{48,56},{56,48},{64,72... | collective-permute-start | bytes 786440 | tf_op jit(solution)/shard_map/ppermute | solution.py:223

commit v6 on v5

--- a/solution.py
+++ b/solution.py
@@ -19,7 +19,7 @@
 PACK = 512
 HALF = 128
 MAXS = 16
-BATCH = 4
+BATCHES = ((0, 2), (2, 5), (5, 8))
 BLOCKS = 8
 epsilon = 1e-06
 
@@ -44,10 +44,18 @@
     return high, (values - high.astype(jnp.float32)).astype(jnp.bfloat16)
 
 
+def product(left, right, dims):
+    return lax.dot_general(left, right, (dims, ((), ())), preferred_element_type=jnp.float32)
+
+
+def total(values):
+    return jnp.sum(jnp.sum(values, axis=0, keepdims=True), axis=1, keepdims=True)
+
+
 def dot(left, right, dims=NN):
     lefts = jnp.concatenate([left[0], left[0], left[1]], axis=1)
     rights = jnp.concatenate([right[0], right[1], right[0]], axis=dims[1][0])
-    return lax.dot_general(lefts, rights, (dims, ((), ())), preferred_element_type=jnp.float32)
+    return product(lefts, rights, dims)
 
 
 def trend_projector():
@@ -70,8 +78,8 @@
         copy.start()
     table.wait()
     stores = []
-    for start in range(0, LOCAL, BATCH):
-        frames = range(start, start + BATCH)
+    for start, stop in BATCHES:
+        frames = range(start, stop)
         for frame in frames:
             copies[frame].wait()
         for frame in frames:
@@ -128,7 +136,9 @@
     extra = jnp.where(lane == HALF // 2, jnp.sum(numerator, axis=1, keepdims=True), jnp.sum(picture * picture))
     extra = jnp.where(lane == HALF // 2 + 1, jnp.sum(energy, axis=1, keepdims=True), extra)
     extra = jnp.where(lane < HALF // 2, gram_ref[:, HALF:], extra)
-    cross = dot((high_ref[...], low_ref[...]), (spatial_high_ref[...], spatial_low_ref[...]), NT)
+    cross = product(high_ref[...], spatial_high_ref[...], NT) + (
+        product(high_ref[...], spatial_low_ref[...], NT) + product(low_ref[...], spatial_high_ref[...], NT)
+    )
     upper = upper_ref[:1, :1] > 0.0
     for columns, values in (
         (slice(0, HALF), gram_ref[:, :HALF]), (slice(HALF, COMP), extra), (slice(COMP, PACK), cross)
@@ -142,18 +152,18 @@
 
 
 def spread_kernel(in_ref, out_ref):
-    total = jnp.sum(in_ref[...], axis=0)
-    out_ref[...] = jnp.broadcast_to(total[None], out_ref.shape)
+    rows = jnp.sum(in_ref[...], axis=0)
+    out_ref[...] = jnp.broadcast_to(rows[None], out_ref.shape)
 
 
 def weigh_kernel(in_ref, out_ref):
-    total = jnp.sum(in_ref[...], axis=0)
+    rows = jnp.sum(in_ref[...], axis=0)
     first = HALF + HALF // 2
-    energy = total[:, first + 1:first + 2] * total[:, first + 2:first + 3]
-    weight = total[:, first:first + 1] / jnp.sqrt(energy + epsilon)
+    energy = rows[:, first + 1:first + 2] * rows[:, first + 2:first + 3]
+    weight = rows[:, first:first + 1] / jnp.sqrt(energy + epsilon)
     column = lax.broadcasted_iota(jnp.int32, (LOCAL, PACK), 1)
-    total = jnp.where(column >= COMP, total * weight, jnp.where(column == first, weight, total))
-    out_ref[...] = jnp.broadcast_to(total[None], out_ref.shape)
+    rows = jnp.where(column >= COMP, rows * weight, jnp.where(column == first, weight, rows))
+    out_ref[...] = jnp.broadcast_to(rows[None], out_ref.shape)
 
 
 def step_kernel(upper_ref, mine_ref, other_ref, temporal_ref, trend_ref, mask_ref,
@@ -176,31 +186,36 @@
     trend = split(trend_ref[...])
     temporal = temporal_ref[...]
     grad = dot(split(temporal), gram) + dot(trend, split(cross)) - cross
-    step = jnp.sum(grad * grad) / (jnp.sum(grad * dot(split(grad), gram)) + epsilon)
+    step = total(grad * grad) / (total(grad * dot(split(grad), gram)) + epsilon)
     temporal = jnp.maximum(temporal - step * grad, 0.0)
     out_ref[...] = temporal
     flipped = jnp.transpose(temporal)
     parts = split(flipped)
-    temporal_gram = split(dot(parts, parts, NT))
+    mixed = product(parts[0], parts[1], NT)
+    temporal_gram = split(product(parts[0], parts[0], NT) + (mixed + jnp.transpose(mixed)))
     weight_row = jnp.transpose(jnp.broadcast_to(weight, (FRAMES, 128)))[:1]
     projector = split((flipped - dot(parts, trend)) * weight_row)
     spatial_grad = (
         dot(temporal_gram, (spatial_high_ref[...], spatial_low_ref[...]))
         - dot(projector, (high_ref[...], low_ref[...]))
-    ) * mask_ref[:, :1]
+    )
+    mask = mask_ref[...]
+    spatial_grad = jnp.concatenate(
+        [spatial_grad[:, row * WIDTH:(row + 1) * WIDTH] * mask for row in range(ROWS)], axis=1
+    )
     for row in range(ROWS):
         grad_ref[pl.ds(row, COMP, stride=ROWS), :] = spatial_grad[:, row * WIDTH:(row + 1) * WIDTH]
-    square = jnp.sum(spatial_grad * spatial_grad)
-    curve = jnp.sum(spatial_grad * dot(temporal_gram, split(spatial_grad)))
+    square = total(spatial_grad * spatial_grad)
+    curve = total(spatial_grad * dot(temporal_gram, split(spatial_grad)))
     lane = lax.broadcasted_iota(jnp.int32, sums_ref.shape, 2)
     sums_ref[...] = jnp.where(lane == 0, square, jnp.where(lane == 1, curve, 0.0))
 
 
 def final_kernel(sums_ref, stack_ref, grad_ref, out_hbm, out_ref, sems):
-    totals = jnp.sum(jnp.sum(sums_ref[...], axis=0), axis=0, keepdims=True)
-    lane = lax.broadcasted_iota(jnp.int32, totals.shape, 1)
-    square = jnp.sum(jnp.where(lane == 0, totals, 0.0), axis=1, keepdims=True)
-    curve = jnp.sum(jnp.where(lane == 1, totals, 0.0), axis=1, keepdims=True)
+    sums = jnp.sum(sums_ref[...], axis=0)
+    lane = lax.broadcasted_iota(jnp.int32, sums.shape, 1)
+    square = total(jnp.where(lane == 0, sums, 0.0))
+    curve = total(jnp.where(lane == 1, sums, 0.0))
     step = square / (curve + epsilon)
     size = COMP * ROWS // BLOCKS
     stores = []
@@ -274,17 +289,17 @@
     mine = exchange(spread(weigh_kernel, "weigh", part, GROUP // 2), "frames", chips).reshape(HALF, PACK)
     temporal, grad, sums = call(
         step_kernel, "steps",
-        (f32(FRAMES, COMP), f32(COMP * ROWS, WIDTH), f32(GROUP * PLANES, 1, 128)),
+        (f32(FRAMES, COMP), f32(COMP * ROWS, WIDTH), f32(GROUP, PLANES, 128)),
         [VMEM] * 10,
     )(upper, mine, swap(mine), temporal_init, jnp.asarray(trend_projector()), mask,
       spatial_high, spatial_low, high, low)
-    sums = exchange(sums, ("frames", "planes")).reshape(GROUP, PLANES, 128)
+    sums = exchange(sums.reshape(GROUP * PLANES, 1, 128), ("frames", "planes"))
     spatial = call(
         final_kernel, "update", f32(COMP * ROWS, WIDTH), [VMEM] * 3, out_specs=HBM,
         scratch_shapes=[
             pltpu.VMEM((COMP * ROWS, WIDTH), jnp.float32), pltpu.SemaphoreType.DMA((BLOCKS,)),
         ],
-    )(sums, stack, grad)
+    )(sums.reshape(GROUP, PLANES, 128), stack, grad)
     return (temporal, spatial.reshape(COMP, 1, TILE))
 
 

time: 97.8 us -> 97.5 us (level)
  no operation moved by 1% of the time
where the time goes in v6:
time: 97.5 us; the launch traced here: 97.1 us
  blocking collectives  56.1 us (58%)
  waiting for transfers between devices  14.8 us (15%)
  starting transfers between devices  12.9 us (13%)
  Pallas kernels  9.43 us (10%)
  local copies, waits for them, and re-layouts  3.04 us (3%)
    all_to_all x4, blocking collectives, exchange(): lax.all_to_all(values, axes, split_axis=0, concat_axis=0, axis_index_grou...  56.1 us
    all_to_all x1, waiting for transfers between devices, exchange(): lax.all_to_all(values, axes, split_axis=0, concat_axis=0, axis_index_grou...  12.4 us
    all_to_all x1, starting transfers between devices, exchange(): lax.all_to_all(values, axes, split_axis=0, concat_axis=0, axis_index_grou...  8.6 us
    ppermute x2, starting transfers between devices, swap(): lax.ppermute(values, 'frames', [(index, index ^ 1) for index in range(GRO...  4.33 us
    pallas_call x1, Pallas kernels, body(): call(step_kernel, 'steps', (f32(FRAMES, COMP), f32(COMP * ROWS, WIDTH), f...  3.11 us
    unnamed x10, local copies, waits for them, and re-layouts  3.04 us
    pallas_call x1, Pallas kernels, body(): call(register_kernel, 'register', f32(GROUP, LOCAL, ROWS, WIDTH), [HBM, H...  2.46 us
    ppermute x2, waiting for transfers between devices, swap(): lax.ppermute(values, 'frames', [(index, index ^ 1) for index in range(GRO...  2.32 us
  transfers between devices with their start and end apart: 3, of which 3 were waited for; matrix products, arithmetic and copies ran while one was open for 0% of the time, Pallas kernels for 2%

profile of v6, /device:TPU:1, one launch (start us, length us, event | category | flops | bytes accessed | tf_op | source)
XLA Modules:
  0.0 97.1 jit_solution(4399297075129712036)
XLA Ops:
  0.6 2.5 %register.1 = f32[32,8,8,128]{3,2,1,0:T(8,128)} custom-call(s32[2,8]{1,0:T(2,128)} %bitcast.29, f32[8,256,128]{2,1,0:T(8,128)} %bitcast.28), custom_call_target="tpu_custom_call" | custom-call | tf_op jit(solution)/shard_map/register/pallas_call | solution.py:255
  3.1 8.6 %all-to-all-start = ((f32[32,8,8,128]{3,2,1,0:T(8,128)}), f32[32,8,8,128]{3,2,1,0:T(8,128)S(1)}, u32[]{:S(2)}, u32[]{:S(2)}) async-start(f32[32,8,8,128]{3,2,1,0:T(8,128)} %register.1), calls=%async_computation | async-start | bytes 2097152 | tf_op jit(solution)/shard_map/all_to_all | solution.py:232
  11.7 0.1 pad_add_fusion.place_ref
  11.8 0.0 copy-start.2
  11.8 1.2 %copy-done.2 = f32[256,1,1024]{2,1,0:T(1,128)S(1)} copy-done((f32[256,1,1024]{2,1,0:T(1,128)S(1)}, f32[256,1,1024]{2,1,0:T(1,128)}, u32[]{:S(2)}) %copy-start.2) | copy-done | bytes 1048600
  13.0 0.0 copy-start.3
  13.0 0.9 copy-done.3
  13.9 0.0 copy-start.4
  13.9 0.9 copy-done.4
  14.8 1.6 %spatial.1 = (f32[2048,128]{1,0:T(8,128)S(1)}, bf16[256,1024]{1,0:T(8,128)(2,1)S(1)}, bf16[256,1024]{1,0:T(8,128)(2,1)S(1)}, f32[256,128]{1,0:T(8,128)S(1)}, f32...) custom-call(s32[3]{0:T(128)S(1)} %pad_add_fusion.place_ref, f32[2048,128]{1,0:T(8,128)S(1)} %bitcast.24, ...), custom_call_target="tpu_custom_call" | custom-call | flops 402653184 | bytes 4194304 | tf_op jit(solution)/shard_map/spatial/pallas_call | solution.py:269
  16.4 12.4 %all-to-all-done = f32[32,8,8,128]{3,2,1,0:T(8,128)S(1)} async-done(((f32[32,8,8,128]{3,2,1,0:T(8,128)}), f32[32,8,8,128]{3,2,1,0:T(8,128)S(1)}, u32[]{:S(2)}, u32[]{:S(2)}) %all-to-all-start) | async-done | bytes 1048608 | tf_op jit(solution)/shard_map/all_to_all | solution.py:232
  28.9 0.8 cross.1
  29.6 0.5 collective-permute-start
  30.1 1.2 %collective-permute-done.right_ref = f32[128,512]{1,0:T(8,128)S(1)} collective-permute-done((f32[128,512]{1,0:T(8,128)S(1)}, f32[128,512]{1,0:T(8,128)S(1)}, u32[]{:S(2)}, u32[]{:S(2)}) %collective-permute-start) | collective-permute-done | bytes 262176 | tf_op jit(solution)/shard_map/ppermute | solution.py:238
  31.3 11.4 %all_to_all.25.in_ref = f32[16,8,512]{2,1,0:T(8,128)S(1)} all-to-all(f32[16,8,512]{2,1,0:T(8,128)S(1)} %bitcast.21), channel_id=1, replica_groups={{0,16,32,48,64,80,96,112,128,144,160,176,192,208,224,240},{8,24,40,56,7..., dimensions={0} | all-to-all | bytes 524288 | tf_op jit(solution)/shard_map/all_to_all | solution.py:232
  42.8 15.9 %all_to_all.26.in_ref = f32[8,8,512]{2,1,0:T(8,128)S(1)} all-to-all(f32[8,8,512]{2,1,0:T(8,128)S(1)} %spread.1), channel_id=1, replica_groups=mesh['frames'=32,'planes'=8] {'planes'}, dimensions={0} | all-to-all | bytes 262144 | tf_op jit(solution)/shard_map/all_to_all | solution.py:232
  58.7 0.2 weigh.1
  59.0 0.0 copy-start
  59.0 0.0 copy-start.1
  59.0 10.5 %all_to_all.27 = f32[16,8,512]{2,1,0:T(8,128)S(1)} all-to-all(f32[16,8,512]{2,1,0:T(8,128)S(1)} %weigh.1), channel_id=1, replica_groups={{0,16,32,48,64,80,96,112,128,144,160,176,192,208,224,240},{8,24,40,56,7..., dimensions={0} | all-to-all | bytes 524288 | tf_op jit(solution)/shard_map/all_to_all | solution.py:232
  69.5 3.9 %collective-permute-start.1 = (f32[128,512]{1,0:T(8,128)S(1)}, f32[128,512]{1,0:T(8,128)S(1)}, u32[]{:S(2)}, u32[]{:S(2)}) collective-permute-start(f32[128,512]{1,0:T(8,128)S(1)} %bitcast.19), channel_id=1, source_target_pairs={{0,8},{8,0},{16,24},{24,16},{32,40},{40,32},{48,56},{56,48},{64,72... | collective-permute-start | bytes 786440 | tf_op jit(solution)/shard_map/ppermute | solution.py:238
  73.4 1.2 %collective-permute-done.1.other_ref = f32[128,512]{1,0:T(8,128)S(1)} collective-permute-done((f32[128,512]{1,0:T(8,128)S(1)}, f32[128,512]{1,0:T(8,128)S(1)}, u32[]{:S(2)}, u32[]{:S(2)}) %collective-permute-start.1) | collective-permute-done | bytes 262176 | tf_op jit(solution)/shard_map/ppermute | solution.py:238
  74.6 0.0 copy-done
  74.6 0.0 copy-done.1
  74.6 3.1 %steps.1 = (f32[256,256]{1,0:T(8,128)}, f32[2048,128]{1,0:T(8,128)S(1)}, f32[32,8,128]{2,1,0:T(8,128)S(1)}) custom-call(f32[8,128]{1,0:T(8,128)S(1)} %get-tuple-element.16.upper_ref, f32[128,512]{1,0:T(8,128)S(1)} %bitcast.20, f32[128,512]{1,0:T(8,128)S(1)} %collective-permute-done.1.other_ref, f32[256,256]{1,0:T(8,128)S(1)} %copy-done, ...), custom_call_target="tpu_custom_call" | custom-call | tf_op jit(solution)/shard_map/steps/pallas_call | solution.py:290
  77.7 18.2 %all_to_all.28 = f32[256,1,128]{2,1,0:T(1,128)S(1)} all-to-all(f32[256,1,128]{2,1,0:T(1,128)S(1)} %bitcast.23), channel_id=1, replica_groups=mesh['frames'=32,'planes'=8] {'frames','planes'}, dimensions={0} | all-to-all | bytes 262144 | tf_op jit(solution)/shard_map/all_to_all | solution.py:232
  95.9 1.2 %update.1 = f32[2048,128]{1,0:T(8,128)} custom-call(f32[32,8,128]{2,1,0:T(8,128)S(1)} %bitcast.22, f32[2048,128]{1,0:T(8,128)S(1)} %get-tuple-element.28.stack_ref, f32[2048,128]{1,0:T(8,128)S(1)} %get-tuple-element.29.grad_ref), custom_call_target="tpu_custom_call" | custom-call | tf_op jit(solution)/shard_map/update/pallas_call | solution.py:297
  (2 shorter events, 0.1 us)
Async XLA Ops:
  3.1 25.8 %all-to-all-start = ((f32[32,8,8,128]{3,2,1,0:T(8,128)}), f32[32,8,8,128]{3,2,1,0:T(8,128)S(1)}, u32[]{:S(2)}, u32[]{:S(2)}) async-start(f32[32,8,8,128]{3,2,1,0:T(8,128)} %register.1), calls=%async_computation | async-start | bytes 2097152 | tf_op jit(solution)/shard_map/all_to_all | solution.py:232
  11.8 1.2 %copy-start.2 = (f32[256,1,1024]{2,1,0:T(1,128)S(1)}, f32[256,1,1024]{2,1,0:T(1,128)}, u32[]{:S(2)}) copy-start(f32[256,1,1024]{2,1,0:T(1,128)} %param.12) | copy-start | bytes 3145732
  13.0 0.9 copy-start.3
  13.9 0.9 copy-start.4
  29.6 1.6 %collective-permute-start = (f32[128,512]{1,0:T(8,128)S(1)}, f32[128,512]{1,0:T(8,128)S(1)}, u32[]{:S(2)}, u32[]{:S(2)}) collective-permute-start(f32[128,512]{1,0:T(8,128)S(1)} %get-tuple-element.22), channel_id=1, source_target_pairs={{0,8},{8,0},{16,24},{24,16},{32,40},{40,32},{48,56},{56,48},{64,72... | collective-permute-start | bytes 786440 | tf_op jit(solution)/shard_map/ppermute | solution.py:238
  59.0 15.6 %copy-start = (f32[256,256]{1,0:T(8,128)S(1)}, f32[256,256]{1,0:T(8,128)}, u32[]{:S(2)}) copy-start(f32[256,256]{1,0:T(8,128)} %temporal_ref.1) | copy-start | bytes 786436
  59.0 15.6 %copy-start.1 = (f32[256,256]{1,0:T(8,128)S(1)}, f32[256,256]{1,0:T(8,128)}, u32[]{:S(2)}) copy-start(f32[256,256]{1,0:T(8,128)} %constant.13.clone.trend_ref) | copy-start | bytes 786436
  69.5 5.0 %collective-permute-start.1 = (f32[128,512]{1,0:T(8,128)S(1)}, f32[128,512]{1,0:T(8,128)S(1)}, u32[]{:S(2)}, u32[]{:S(2)}) collective-permute-start(f32[128,512]{1,0:T(8,128)S(1)} %bitcast.19), channel_id=1, source_target_pairs={{0,8},{8,0},{16,24},{24,16},{32,40},{40,32},{48,56},{56,48},{64,72... | collective-permute-start | bytes 786440 | tf_op jit(solution)/shard_map/ppermute | solution.py:238

commit v7 on v6

--- a/solution.py
+++ b/solution.py
@@ -22,6 +22,11 @@
 BATCHES = ((0, 2), (2, 5), (5, 8))
 BLOCKS = 8
 epsilon = 1e-06
+
+GRID = np.arange(GROUP * PLANES).reshape(4, 4, 2, PLANES)
+PLANE = (GRID[..., 0] // PLANES).transpose(1, 0, 2).flatten().tolist()
+CHIPS = (GRID[..., 0] // PLANES).transpose(2, 1, 0).reshape(2, 16).tolist()
+ALL = GRID.transpose(3, 2, 0, 1).flatten().tolist()
 
 VMEM = pl.BlockSpec(memory_space=pltpu.VMEM)
 SMEM = pl.BlockSpec(memory_space=pltpu.SMEM)
@@ -90,7 +95,8 @@
             wide[pl.ds(MAXS + HEIGHT, MAXS), :] = picture[:MAXS]
         for frame in frames:
             moved = wide_ref[frame, pl.ds(MAXS - shift_ref[0, frame], HEIGHT), :]
-            moved_ref[frame] = moved.reshape(GROUP, ROWS, WIDTH)
+            for slot, block in enumerate(PLANE):
+                moved_ref[frame, slot] = moved[block * ROWS:(block + 1) * ROWS]
         for frame in frames:
             store = pltpu.make_async_copy(moved_ref.at[frame], out_hbm.at[:, frame], moved_sem.at[frame])
             store.start()
@@ -128,7 +134,10 @@
     energy = jnp.zeros((FRAMES, WIDTH), jnp.float32)
     for row in range(ROWS):
         columns = slice(row * WIDTH, (row + 1) * WIDTH)
-        series = series_ref[pl.ds(row, FRAMES, stride=ROWS), :]
+        series = jnp.concatenate([
+            series_ref[pl.ds(PLANE.index(block) * LOCAL * ROWS + row, LOCAL, stride=ROWS), :]
+            for block in range(GROUP)
+        ], axis=0)
         high_ref[:, columns], low_ref[:, columns] = split(series)
         numerator += series * picture[row:row + 1]
         energy += series * series
@@ -264,7 +273,7 @@
             pltpu.SemaphoreType.DMA((LOCAL,)),
         ],
     )(shift_table, movie)
-    series = exchange(payload, "frames").reshape(FRAMES * ROWS, WIDTH)
+    series = exchange(payload, "frames", [PLANE]).reshape(FRAMES * ROWS, WIDTH)
     spatial = spatial_init.reshape(COMP * ROWS, WIDTH)
     stack, spatial_high, spatial_low, mask, gram, picture, upper = call(
         spatial_kernel, "spatial",
@@ -282,18 +291,17 @@
     def spread(kernel, name, values, copies):
         return call(kernel, name, f32(copies, *values.shape[1:]), [VMEM])(values)
 
-    chips = [list(range(core, GROUP, 2)) for core in range(2)]
     part = call(add_kernel, "pair", f32(HALF, PACK), [VMEM] * 2)(keep, swap(give))
-    part = exchange(part.reshape(GROUP // 2, LOCAL, PACK), "frames", chips)
+    part = exchange(part.reshape(GROUP // 2, LOCAL, PACK), "frames", CHIPS)
     part = exchange(spread(spread_kernel, "spread", part, PLANES), "planes")
-    mine = exchange(spread(weigh_kernel, "weigh", part, GROUP // 2), "frames", chips).reshape(HALF, PACK)
+    mine = exchange(spread(weigh_kernel, "weigh", part, GROUP // 2), "frames", CHIPS).reshape(HALF, PACK)
     temporal, grad, sums = call(
         step_kernel, "steps",
         (f32(FRAMES, COMP), f32(COMP * ROWS, WIDTH), f32(GROUP, PLANES, 128)),
         [VMEM] * 10,
     )(upper, mine, swap(mine), temporal_init, jnp.asarray(trend_projector()), mask,
       spatial_high, spatial_low, high, low)
-    sums = exchange(sums.reshape(GROUP * PLANES, 1, 128), ("frames", "planes"))
+    sums = exchange(sums.reshape(GROUP * PLANES, 1, 128), ("frames", "planes"), [ALL])
     spatial = call(
         final_kernel, "update", f32(COMP * ROWS, WIDTH), [VMEM] * 3, out_specs=HBM,
         scratch_shapes=[

time: 97.5 us -> 97.4 us (level)
  no operation moved by 1% of the time
where the time goes in v7:
time: 97.4 us; the launch traced here: 97 us
  blocking collectives  55.8 us (57%)
  waiting for transfers between devices  14.7 us (15%)
  starting transfers between devices  13.2 us (14%)
  Pallas kernels  9.43 us (10%)
  local copies, waits for them, and re-layouts  3.04 us (3%)
    all_to_all x4, blocking collectives, exchange(): lax.all_to_all(values, axes, split_axis=0, concat_axis=0, axis_index_grou...  55.8 us
    all_to_all x1, waiting for transfers between devices, exchange(): lax.all_to_all(values, axes, split_axis=0, concat_axis=0, axis_index_grou...  12.2 us
    all_to_all x1, starting transfers between devices, exchange(): lax.all_to_all(values, axes, split_axis=0, concat_axis=0, axis_index_grou...  8.6 us
    ppermute x2, starting transfers between devices, swap(): lax.ppermute(values, 'frames', [(index, index ^ 1) for index in range(GRO...  4.61 us
    pallas_call x1, Pallas kernels, body(): call(step_kernel, 'steps', (f32(FRAMES, COMP), f32(COMP * ROWS, WIDTH), f...  3.11 us
    unnamed x10, local copies, waits for them, and re-layouts  3.04 us
    ppermute x2, waiting for transfers between devices, swap(): lax.ppermute(values, 'frames', [(index, index ^ 1) for index in range(GRO...  2.56 us
    pallas_call x1, Pallas kernels, body(): call(register_kernel, 'register', f32(GROUP, LOCAL, ROWS, WIDTH), [HBM, H...  2.46 us
  transfers between devices with their start and end apart: 3, of which 3 were waited for; matrix products, arithmetic and copies ran while one was open for 0% of the time, Pallas kernels for 2%

profile of v7, /device:TPU:1, one launch (start us, length us, event | category | flops | bytes accessed | tf_op | source)
XLA Modules:
  0.0 97.0 jit_solution(2086664357355723832)
XLA Ops:
  0.6 2.5 %register.1 = f32[32,8,8,128]{3,2,1,0:T(8,128)} custom-call(s32[2,8]{1,0:T(2,128)} %bitcast.29, f32[8,256,128]{2,1,0:T(8,128)} %bitcast.28), custom_call_target="tpu_custom_call" | custom-call | tf_op jit(solution)/shard_map/register/pallas_call | solution.py:264
  3.1 8.6 %all-to-all-start = ((f32[32,8,8,128]{3,2,1,0:T(8,128)}), f32[32,8,8,128]{3,2,1,0:T(8,128)S(1)}, u32[]{:S(2)}, u32[]{:S(2)}) async-start(f32[32,8,8,128]{3,2,1,0:T(8,128)} %register.1), calls=%async_computation | async-start | bytes 2097152 | tf_op jit(solution)/shard_map/all_to_all | solution.py:241
  11.7 0.1 pad_add_fusion.place_ref
  11.8 0.0 copy-start.2
  11.8 1.2 %copy-done.2 = f32[256,1,1024]{2,1,0:T(1,128)S(1)} copy-done((f32[256,1,1024]{2,1,0:T(1,128)S(1)}, f32[256,1,1024]{2,1,0:T(1,128)}, u32[]{:S(2)}) %copy-start.2) | copy-done | bytes 1048600
  13.0 0.0 copy-start.3
  13.0 0.9 copy-done.3
  13.9 0.0 copy-start.4
  13.9 0.9 copy-done.4
  14.8 1.6 %spatial.1 = (f32[2048,128]{1,0:T(8,128)S(1)}, bf16[256,1024]{1,0:T(8,128)(2,1)S(1)}, bf16[256,1024]{1,0:T(8,128)(2,1)S(1)}, f32[256,128]{1,0:T(8,128)S(1)}, f32...) custom-call(s32[3]{0:T(128)S(1)} %pad_add_fusion.place_ref, f32[2048,128]{1,0:T(8,128)S(1)} %bitcast.24, ...), custom_call_target="tpu_custom_call" | custom-call | flops 402653184 | bytes 4194304 | tf_op jit(solution)/shard_map/spatial/pallas_call | solution.py:278
  16.4 12.2 %all-to-all-done = f32[32,8,8,128]{3,2,1,0:T(8,128)S(1)} async-done(((f32[32,8,8,128]{3,2,1,0:T(8,128)}), f32[32,8,8,128]{3,2,1,0:T(8,128)S(1)}, u32[]{:S(2)}, u32[]{:S(2)}) %all-to-all-start) | async-done | bytes 1048608 | tf_op jit(solution)/shard_map/all_to_all | solution.py:241
  28.6 0.8 cross.1
  29.4 0.2 collective-permute-start
  29.6 1.4 %collective-permute-done.right_ref = f32[128,512]{1,0:T(8,128)S(1)} collective-permute-done((f32[128,512]{1,0:T(8,128)S(1)}, f32[128,512]{1,0:T(8,128)S(1)}, u32[]{:S(2)}, u32[]{:S(2)}) %collective-permute-start) | collective-permute-done | bytes 262176 | tf_op jit(solution)/shard_map/ppermute | solution.py:247
  31.0 10.6 %all_to_all.25.in_ref = f32[16,8,512]{2,1,0:T(8,128)S(1)} all-to-all(f32[16,8,512]{2,1,0:T(8,128)S(1)} %bitcast.21), channel_id=1, replica_groups={{0,64,128,192,16,80,144,208,32,96,160,224,48,112,176,240},{8,72,136,200..., dimensions={0} | all-to-all | bytes 524288 | tf_op jit(solution)/shard_map/all_to_all | solution.py:241
  41.7 16.0 %all_to_all.26.in_ref = f32[8,8,512]{2,1,0:T(8,128)S(1)} all-to-all(f32[8,8,512]{2,1,0:T(8,128)S(1)} %spread.1), channel_id=1, replica_groups=mesh['frames'=32,'planes'=8] {'planes'}, dimensions={0} | all-to-all | bytes 262144 | tf_op jit(solution)/shard_map/all_to_all | solution.py:241
  57.7 0.2 weigh.1
  57.9 0.0 copy-start
  58.0 0.0 copy-start.1
  58.0 10.9 %all_to_all.27 = f32[16,8,512]{2,1,0:T(8,128)S(1)} all-to-all(f32[16,8,512]{2,1,0:T(8,128)S(1)} %weigh.1), channel_id=1, replica_groups={{0,64,128,192,16,80,144,208,32,96,160,224,48,112,176,240},{8,72,136,200..., dimensions={0} | all-to-all | bytes 524288 | tf_op jit(solution)/shard_map/all_to_all | solution.py:241
  68.8 4.4 %collective-permute-start.1 = (f32[128,512]{1,0:T(8,128)S(1)}, f32[128,512]{1,0:T(8,128)S(1)}, u32[]{:S(2)}, u32[]{:S(2)}) collective-permute-start(f32[128,512]{1,0:T(8,128)S(1)} %bitcast.19), channel_id=1, source_target_pairs={{0,8},{8,0},{16,24},{24,16},{32,40},{40,32},{48,56},{56,48},{64,72... | collective-permute-start | bytes 786440 | tf_op jit(solution)/shard_map/ppermute | solution.py:247
  73.2 1.2 %collective-permute-done.1.other_ref = f32[128,512]{1,0:T(8,128)S(1)} collective-permute-done((f32[128,512]{1,0:T(8,128)S(1)}, f32[128,512]{1,0:T(8,128)S(1)}, u32[]{:S(2)}, u32[]{:S(2)}) %collective-permute-start.1) | collective-permute-done | bytes 262176 | tf_op jit(solution)/shard_map/ppermute | solution.py:247
  74.4 0.0 copy-done
  74.4 0.0 copy-done.1
  74.4 3.1 %steps.1 = (f32[256,256]{1,0:T(8,128)}, f32[2048,128]{1,0:T(8,128)S(1)}, f32[32,8,128]{2,1,0:T(8,128)S(1)}) custom-call(f32[8,128]{1,0:T(8,128)S(1)} %get-tuple-element.16.upper_ref, f32[128,512]{1,0:T(8,128)S(1)} %bitcast.20, f32[128,512]{1,0:T(8,128)S(1)} %collective-permute-done.1.other_ref, f32[256,256]{1,0:T(8,128)S(1)} %copy-done, ...), custom_call_target="tpu_custom_call" | custom-call | tf_op jit(solution)/shard_map/steps/pallas_call | solution.py:298
  77.5 18.3 %all_to_all.28 = f32[256,1,128]{2,1,0:T(1,128)S(1)} all-to-all(f32[256,1,128]{2,1,0:T(1,128)S(1)} %bitcast.23), channel_id=1, replica_groups={{0,16,32,48,64,80,96,112,128,144,160,176,192,208,224,240,8,24,40,56,72,..., dimensions={0} | all-to-all | bytes 262144 | tf_op jit(solution)/shard_map/all_to_all | solution.py:241
  95.8 1.2 %update.1 = f32[2048,128]{1,0:T(8,128)} custom-call(f32[32,8,128]{2,1,0:T(8,128)S(1)} %bitcast.22, f32[2048,128]{1,0:T(8,128)S(1)} %get-tuple-element.28.stack_ref, f32[2048,128]{1,0:T(8,128)S(1)} %get-tuple-element.29.grad_ref), custom_call_target="tpu_custom_call" | custom-call | tf_op jit(solution)/shard_map/update/pallas_call | solution.py:305
  (2 shorter events, 0.1 us)
Async XLA Ops:
  3.1 25.5 %all-to-all-start = ((f32[32,8,8,128]{3,2,1,0:T(8,128)}), f32[32,8,8,128]{3,2,1,0:T(8,128)S(1)}, u32[]{:S(2)}, u32[]{:S(2)}) async-start(f32[32,8,8,128]{3,2,1,0:T(8,128)} %register.1), calls=%async_computation | async-start | bytes 2097152 | tf_op jit(solution)/shard_map/all_to_all | solution.py:241
  11.8 1.2 %copy-start.2 = (f32[256,1,1024]{2,1,0:T(1,128)S(1)}, f32[256,1,1024]{2,1,0:T(1,128)}, u32[]{:S(2)}) copy-start(f32[256,1,1024]{2,1,0:T(1,128)} %param.12) | copy-start | bytes 3145732
  13.0 0.9 copy-start.3
  13.9 0.9 copy-start.4
  29.4 1.6 %collective-permute-start = (f32[128,512]{1,0:T(8,128)S(1)}, f32[128,512]{1,0:T(8,128)S(1)}, u32[]{:S(2)}, u32[]{:S(2)}) collective-permute-start(f32[128,512]{1,0:T(8,128)S(1)} %get-tuple-element.22), channel_id=1, source_target_pairs={{0,8},{8,0},{16,24},{24,16},{32,40},{40,32},{48,56},{56,48},{64,72... | collective-permute-start | bytes 786440 | tf_op jit(solution)/shard_map/ppermute | solution.py:247
  57.9 16.4 %copy-start = (f32[256,256]{1,0:T(8,128)S(1)}, f32[256,256]{1,0:T(8,128)}, u32[]{:S(2)}) copy-start(f32[256,256]{1,0:T(8,128)} %temporal_ref.1) | copy-start | bytes 786436
  58.0 16.4 %copy-start.1 = (f32[256,256]{1,0:T(8,128)S(1)}, f32[256,256]{1,0:T(8,128)}, u32[]{:S(2)}) copy-start(f32[256,256]{1,0:T(8,128)} %constant.13.clone.trend_ref) | copy-start | bytes 786436
  68.8 5.5 %collective-permute-start.1 = (f32[128,512]{1,0:T(8,128)S(1)}, f32[128,512]{1,0:T(8,128)S(1)}, u32[]{:S(2)}, u32[]{:S(2)}) collective-permute-start(f32[128,512]{1,0:T(8,128)S(1)} %bitcast.19), channel_id=1, source_target_pairs={{0,8},{8,0},{16,24},{24,16},{32,40},{40,32},{48,56},{56,48},{64,72... | collective-permute-start | bytes 786440 | tf_op jit(solution)/shard_map/ppermute | solution.py:247

commit v8 on v6

--- a/solution.py
+++ b/solution.py
@@ -192,7 +192,8 @@
     flipped = jnp.transpose(temporal)
     parts = split(flipped)
     mixed = product(parts[0], parts[1], NT)
-    temporal_gram = split(product(parts[0], parts[0], NT) + (mixed + jnp.transpose(mixed)))
+    temporal_gram_whole = product(parts[0], parts[0], NT) + (mixed + jnp.transpose(mixed))
+    temporal_gram = split(temporal_gram_whole)
     weight_row = jnp.transpose(jnp.broadcast_to(weight, (FRAMES, 128)))[:1]
     projector = split((flipped - dot(parts, trend)) * weight_row)
     spatial_grad = (
@@ -206,7 +207,8 @@
     for row in range(ROWS):
         grad_ref[pl.ds(row, COMP, stride=ROWS), :] = spatial_grad[:, row * WIDTH:(row + 1) * WIDTH]
     square = total(spatial_grad * spatial_grad)
-    curve = total(spatial_grad * dot(temporal_gram, split(spatial_grad)))
+    high, low = split(spatial_grad)
+    curve = total(temporal_gram_whole * (product(high, high, NT) + 2.0 * product(high, low, NT)))
     lane = lax.broadcasted_iota(jnp.int32, sums_ref.shape, 2)
     sums_ref[...] = jnp.where(lane == 0, square, jnp.where(lane == 1, curve, 0.0))
 

time: 97.5 us -> 97.5 us (level)
  no operation moved by 1% of the time
where the time goes in v8:
time: 97.5 us; the launch traced here: 97 us
  blocking collectives  56.1 us (58%)
  waiting for transfers between devices  14.8 us (15%)
  starting transfers between devices  12.9 us (13%)
  Pallas kernels  9.4 us (10%)
  local copies, waits for them, and re-layouts  3.04 us (3%)
    all_to_all x4, blocking collectives, exchange(): lax.all_to_all(values, axes, split_axis=0, concat_axis=0, axis_index_grou...  56.1 us
    all_to_all x1, waiting for transfers between devices, exchange(): lax.all_to_all(values, axes, split_axis=0, concat_axis=0, axis_index_grou...  12.4 us
    all_to_all x1, starting transfers between devices, exchange(): lax.all_to_all(values, axes, split_axis=0, concat_axis=0, axis_index_grou...  8.6 us
    ppermute x2, starting transfers between devices, swap(): lax.ppermute(values, 'frames', [(index, index ^ 1) for index in range(GRO...  4.33 us
    pallas_call x1, Pallas kernels, body(): call(step_kernel, 'steps', (f32(FRAMES, COMP), f32(COMP * ROWS, WIDTH), f...  3.07 us
    unnamed x10, local copies, waits for them, and re-layouts  3.04 us
    pallas_call x1, Pallas kernels, body(): call(register_kernel, 'register', f32(GROUP, LOCAL, ROWS, WIDTH), [HBM, H...  2.46 us
    ppermute x2, waiting for transfers between devices, swap(): lax.ppermute(values, 'frames', [(index, index ^ 1) for index in range(GRO...  2.32 us
  transfers between devices with their start and end apart: 3, of which 3 were waited for; matrix products, arithmetic and copies ran while one was open for 0% of the time, Pallas kernels for 2%

profile of v8, /device:TPU:1, one launch (start us, length us, event | category | flops | bytes accessed | tf_op | source)
XLA Modules:
  0.0 97.0 jit_solution(6660802022893677277)
XLA Ops:
  0.6 2.5 %register.1 = f32[32,8,8,128]{3,2,1,0:T(8,128)} custom-call(s32[2,8]{1,0:T(2,128)} %bitcast.29, f32[8,256,128]{2,1,0:T(8,128)} %bitcast.28), custom_call_target="tpu_custom_call" | custom-call | tf_op jit(solution)/shard_map/register/pallas_call | solution.py:257
  3.1 8.6 %all-to-all-start = ((f32[32,8,8,128]{3,2,1,0:T(8,128)}), f32[32,8,8,128]{3,2,1,0:T(8,128)S(1)}, u32[]{:S(2)}, u32[]{:S(2)}) async-start(f32[32,8,8,128]{3,2,1,0:T(8,128)} %register.1), calls=%async_computation | async-start | bytes 2097152 | tf_op jit(solution)/shard_map/all_to_all | solution.py:234
  11.7 0.1 pad_add_fusion.place_ref
  11.8 0.0 copy-start.2
  11.8 1.2 %copy-done.2 = f32[256,1,1024]{2,1,0:T(1,128)S(1)} copy-done((f32[256,1,1024]{2,1,0:T(1,128)S(1)}, f32[256,1,1024]{2,1,0:T(1,128)}, u32[]{:S(2)}) %copy-start.2) | copy-done | bytes 1048600
  13.0 0.0 copy-start.3
  13.0 0.9 copy-done.3
  13.9 0.0 copy-start.4
  13.9 0.9 copy-done.4
  14.8 1.6 %spatial.1 = (f32[2048,128]{1,0:T(8,128)S(1)}, bf16[256,1024]{1,0:T(8,128)(2,1)S(1)}, bf16[256,1024]{1,0:T(8,128)(2,1)S(1)}, f32[256,128]{1,0:T(8,128)S(1)}, f32...) custom-call(s32[3]{0:T(128)S(1)} %pad_add_fusion.place_ref, f32[2048,128]{1,0:T(8,128)S(1)} %bitcast.24, ...), custom_call_target="tpu_custom_call" | custom-call | flops 402653184 | bytes 4194304 | tf_op jit(solution)/shard_map/spatial/pallas_call | solution.py:271
  16.4 12.4 %all-to-all-done = f32[32,8,8,128]{3,2,1,0:T(8,128)S(1)} async-done(((f32[32,8,8,128]{3,2,1,0:T(8,128)}), f32[32,8,8,128]{3,2,1,0:T(8,128)S(1)}, u32[]{:S(2)}, u32[]{:S(2)}) %all-to-all-start) | async-done | bytes 1048608 | tf_op jit(solution)/shard_map/all_to_all | solution.py:234
  28.9 0.8 cross.1
  29.6 0.5 collective-permute-start
  30.1 1.2 %collective-permute-done.right_ref = f32[128,512]{1,0:T(8,128)S(1)} collective-permute-done((f32[128,512]{1,0:T(8,128)S(1)}, f32[128,512]{1,0:T(8,128)S(1)}, u32[]{:S(2)}, u32[]{:S(2)}) %collective-permute-start) | collective-permute-done | bytes 262176 | tf_op jit(solution)/shard_map/ppermute | solution.py:240
  31.3 11.4 %all_to_all.25.in_ref = f32[16,8,512]{2,1,0:T(8,128)S(1)} all-to-all(f32[16,8,512]{2,1,0:T(8,128)S(1)} %bitcast.21), channel_id=1, replica_groups={{0,16,32,48,64,80,96,112,128,144,160,176,192,208,224,240},{8,24,40,56,7..., dimensions={0} | all-to-all | bytes 524288 | tf_op jit(solution)/shard_map/all_to_all | solution.py:234
  42.8 15.9 %all_to_all.26.in_ref = f32[8,8,512]{2,1,0:T(8,128)S(1)} all-to-all(f32[8,8,512]{2,1,0:T(8,128)S(1)} %spread.1), channel_id=1, replica_groups=mesh['frames'=32,'planes'=8] {'planes'}, dimensions={0} | all-to-all | bytes 262144 | tf_op jit(solution)/shard_map/all_to_all | solution.py:234
  58.7 0.2 weigh.1
  59.0 0.0 copy-start
  59.0 0.0 copy-start.1
  59.0 10.5 %all_to_all.27 = f32[16,8,512]{2,1,0:T(8,128)S(1)} all-to-all(f32[16,8,512]{2,1,0:T(8,128)S(1)} %weigh.1), channel_id=1, replica_groups={{0,16,32,48,64,80,96,112,128,144,160,176,192,208,224,240},{8,24,40,56,7..., dimensions={0} | all-to-all | bytes 524288 | tf_op jit(solution)/shard_map/all_to_all | solution.py:234
  69.5 3.9 %collective-permute-start.1 = (f32[128,512]{1,0:T(8,128)S(1)}, f32[128,512]{1,0:T(8,128)S(1)}, u32[]{:S(2)}, u32[]{:S(2)}) collective-permute-start(f32[128,512]{1,0:T(8,128)S(1)} %bitcast.19), channel_id=1, source_target_pairs={{0,8},{8,0},{16,24},{24,16},{32,40},{40,32},{48,56},{56,48},{64,72... | collective-permute-start | bytes 786440 | tf_op jit(solution)/shard_map/ppermute | solution.py:240
  73.4 1.2 %collective-permute-done.1.other_ref = f32[128,512]{1,0:T(8,128)S(1)} collective-permute-done((f32[128,512]{1,0:T(8,128)S(1)}, f32[128,512]{1,0:T(8,128)S(1)}, u32[]{:S(2)}, u32[]{:S(2)}) %collective-permute-start.1) | collective-permute-done | bytes 262176 | tf_op jit(solution)/shard_map/ppermute | solution.py:240
  74.6 0.0 copy-done
  74.6 0.0 copy-done.1
  74.6 3.1 %steps.1 = (f32[256,256]{1,0:T(8,128)}, f32[2048,128]{1,0:T(8,128)S(1)}, f32[32,8,128]{2,1,0:T(8,128)S(1)}) custom-call(f32[8,128]{1,0:T(8,128)S(1)} %get-tuple-element.16.upper_ref, f32[128,512]{1,0:T(8,128)S(1)} %bitcast.20, f32[128,512]{1,0:T(8,128)S(1)} %collective-permute-done.1.other_ref, f32[256,256]{1,0:T(8,128)S(1)} %copy-done, ...), custom_call_target="tpu_custom_call" | custom-call | tf_op jit(solution)/shard_map/steps/pallas_call | solution.py:292
  77.6 18.2 %all_to_all.28 = f32[256,1,128]{2,1,0:T(1,128)S(1)} all-to-all(f32[256,1,128]{2,1,0:T(1,128)S(1)} %bitcast.23), channel_id=1, replica_groups=mesh['frames'=32,'planes'=8] {'frames','planes'}, dimensions={0} | all-to-all | bytes 262144 | tf_op jit(solution)/shard_map/all_to_all | solution.py:234
  95.9 1.2 %update.1 = f32[2048,128]{1,0:T(8,128)} custom-call(f32[32,8,128]{2,1,0:T(8,128)S(1)} %bitcast.22, f32[2048,128]{1,0:T(8,128)S(1)} %get-tuple-element.28.stack_ref, f32[2048,128]{1,0:T(8,128)S(1)} %get-tuple-element.29.grad_ref), custom_call_target="tpu_custom_call" | custom-call | tf_op jit(solution)/shard_map/update/pallas_call | solution.py:299
  (2 shorter events, 0.1 us)
Async XLA Ops:
  3.1 25.8 %all-to-all-start = ((f32[32,8,8,128]{3,2,1,0:T(8,128)}), f32[32,8,8,128]{3,2,1,0:T(8,128)S(1)}, u32[]{:S(2)}, u32[]{:S(2)}) async-start(f32[32,8,8,128]{3,2,1,0:T(8,128)} %register.1), calls=%async_computation | async-start | bytes 2097152 | tf_op jit(solution)/shard_map/all_to_all | solution.py:234
  11.8 1.2 %copy-start.2 = (f32[256,1,1024]{2,1,0:T(1,128)S(1)}, f32[256,1,1024]{2,1,0:T(1,128)}, u32[]{:S(2)}) copy-start(f32[256,1,1024]{2,1,0:T(1,128)} %param.12) | copy-start | bytes 3145732
  13.0 0.9 copy-start.3
  13.9 0.9 copy-start.4
  29.6 1.6 %collective-permute-start = (f32[128,512]{1,0:T(8,128)S(1)}, f32[128,512]{1,0:T(8,128)S(1)}, u32[]{:S(2)}, u32[]{:S(2)}) collective-permute-start(f32[128,512]{1,0:T(8,128)S(1)} %get-tuple-element.22), channel_id=1, source_target_pairs={{0,8},{8,0},{16,24},{24,16},{32,40},{40,32},{48,56},{56,48},{64,72... | collective-permute-start | bytes 786440 | tf_op jit(solution)/shard_map/ppermute | solution.py:240
  59.0 15.6 %copy-start = (f32[256,256]{1,0:T(8,128)S(1)}, f32[256,256]{1,0:T(8,128)}, u32[]{:S(2)}) copy-start(f32[256,256]{1,0:T(8,128)} %temporal_ref.1) | copy-start | bytes 786436
  59.0 15.6 %copy-start.1 = (f32[256,256]{1,0:T(8,128)S(1)}, f32[256,256]{1,0:T(8,128)}, u32[]{:S(2)}) copy-start(f32[256,256]{1,0:T(8,128)} %constant.13.clone.trend_ref) | copy-start | bytes 786436
  69.5 5.0 %collective-permute-start.1 = (f32[128,512]{1,0:T(8,128)S(1)}, f32[128,512]{1,0:T(8,128)S(1)}, u32[]{:S(2)}, u32[]{:S(2)}) collective-permute-start(f32[128,512]{1,0:T(8,128)S(1)} %bitcast.19), channel_id=1, source_target_pairs={{0,8},{8,0},{16,24},{24,16},{32,40},{40,32},{48,56},{56,48},{64,72... | collective-permute-start | bytes 786440 | tf_op jit(solution)/shard_map/ppermute | solution.py:240
